TPU v7x, 256 devices: a whole 4x4x8 slice. The times are simulated.
256 devices in a mesh: section: 4 (over z_lo, core), seq: 64 (over x, z_hi, y).
Axes of the slice: x: 4, y: 4, z: 8 (z_hi: 4, z_lo: 2; z = z_hi * 2 + z_lo), core: 2. Of those that a mesh axis runs over, the one named last changes fastest.
Arguments:
- stale_out: bfloat16 [4, 2, 4096, 2432], P('section', None, 'seq'), may hold values from -6 to 6
- fresh_latent: bfloat16 [2, 4096, 2432], P(None, 'seq'), may hold values from -6 to 6
- queries: bfloat16 [4, 4096, 4096], P('section', 'seq'), may hold values from -600 to 600
- image_keys: bfloat16 [4, 4096, 4096], P('section', 'seq'), may hold values from -600 to 600
- image_values: bfloat16 [4, 4096, 4096], P('section', 'seq'), may hold values from -6 to 6
- text_keys: bfloat16 [4, 384, 4096], P('section', 'seq'), may hold values from -600 to 600
- text_values: bfloat16 [4, 384, 4096], P('section', 'seq'), may hold values from -12 to 12
- text_count: int32 [2], replicated, may hold values from 1 to 384, as said below
- timesteps: int32 [4, 2], P('section'), may hold values from 0 to 999
- query_gain: float32 [4, 64], P('section'), may hold values from 1 to 2.5
- key_gain: float32 [4, 64], P('section'), may hold values from 1 to 2.5
- out_weight: bfloat16 [4, 2048, 2432], P('section'), may hold values from -0.125 to 0.125
- gate_weight: bfloat16 [4, 256, 2432], P('section', None, 'seq'), may hold values from -0.75 to 0.75
Outputs:
- block_out: bfloat16 [4, 2, 4096, 2432], P('section', None, 'seq')
Inputs may be any that keep to these rules, and one draw needn't show every extreme that they name: `text_count`: some image has all 384 slots live.
All inputs are finite; a program needn't handle non-finite values.
Results may differ from a plain program's by a relative error of at most 0.0056.
Values may be sent and summed in bfloat16 or wider, within the bound.
A program may use at most 128 MiB of HBM per device.

v0:
```python
import math

import jax
import jax.numpy as jnp
from jax import lax
from jax.sharding import PartitionSpec as P

HD = 64
HEADS = 32
TEMB = 256


def shifted_2(array, axis, by):
    count = lax.axis_size(axis)
    pairs = [(i, i + by) for i in range(count) if 0 <= i + by < count]
    return lax.ppermute(array, axis, pairs)


def head_norm(data, gain):
    row_count = data.shape[0]
    pieces = data.reshape(row_count, -1, gain.shape[-1]).astype(jnp.float32)
    factor = lax.rsqrt(jnp.mean(pieces * pieces, axis=-1, keepdims=True) + 1e-06)
    return (pieces * factor * gain).reshape(row_count, -1).astype(jnp.bfloat16)


def attend_item(query_rows, key_rows, value_rows, image_count, text_live):
    query_count, head_size = query_rows.shape
    block_rows = min(512, query_count)
    live_mask = jnp.arange(key_rows.shape[0], dtype=jnp.int32) < image_count + text_live
    blocks = query_rows.reshape(query_count // block_rows, block_rows, head_size)

    def one_block(query_block):
        scores = jnp.einsum(
            "qd,kd->qk", query_block, key_rows, preferred_element_type=jnp.float32
        ) * head_size ** (-0.5)
        weights = jnp.where(live_mask[None, :], jnp.exp(scores), 0.0)
        probs = (weights / jnp.sum(weights, axis=1, keepdims=True)).astype(jnp.bfloat16)
        return jnp.dot(probs, value_rows, preferred_element_type=jnp.float32).astype(jnp.bfloat16)

    return lax.map(one_block, blocks).reshape(query_count, head_size)


def local(
    stale_out,
    fresh_latent,
    queries,
    image_keys,
    image_values,
    text_keys,
    text_values,
    text_count,
    timesteps,
    query_gain,
    key_gain,
    out_weight,
    gate_weight,
):
    seq_count = lax.axis_size("seq")
    shifted = shifted_2(stale_out, "section", 1)
    is_first = lax.axis_index("section") == 0
    block_in = jnp.where(is_first, fresh_latent[None], shifted)[0]
    local_rows = queries.shape[1]
    col_total = queries.shape[2]
    col_span = col_total // seq_count
    item_count = col_span // HD
    image_total = col_total // (HEADS * HD)
    query_scale = query_gain[0]
    key_scale = key_gain[0]
    local_query = queries[0]
    local_key = image_keys[0]
    local_value = image_values[0]
    local_text_key = text_keys[0]
    local_text_value = text_values[0]
    head_query, head_key, head_value = (
        lax.all_to_all(local_query, "seq", split_axis=1, concat_axis=0, tiled=True),
        lax.all_to_all(local_key, "seq", split_axis=1, concat_axis=0, tiled=True),
        lax.all_to_all(local_value, "seq", split_axis=1, concat_axis=0, tiled=True),
    )
    full_text_key, full_text_value = (
        lax.all_gather(local_text_key, "seq", axis=0, tiled=True),
        lax.all_gather(local_text_value, "seq", axis=0, tiled=True),
    )
    col_offset = lax.axis_index("seq") * col_span
    head_text_key = lax.dynamic_slice_in_dim(full_text_key, col_offset, col_span, 1)
    head_text_value = lax.dynamic_slice_in_dim(full_text_value, col_offset, col_span, 1)
    head_query = head_norm(head_query, query_scale)
    head_key = head_norm(head_key, key_scale)
    head_text_key = head_norm(head_text_key, key_scale)
    token_count = head_query.shape[0]
    item_base = lax.axis_index("seq") * item_count

    def one_item(item_index):
        key_rows = jnp.concatenate([head_key, head_text_key], axis=0)
        value_rows = jnp.concatenate([head_value, head_text_value], axis=0)
        text_live = text_count[(item_base + item_index) // HEADS]
        return attend_item(head_query, key_rows, value_rows, token_count, text_live)

    results = lax.map(one_item, jnp.arange(item_count, dtype=jnp.int32))
    attended = jnp.transpose(results, (1, 0, 2)).reshape(token_count, item_count * HD)
    returned = lax.all_to_all(attended, "seq", split_axis=0, concat_axis=1, tiled=True)
    per_image = returned.reshape(local_rows, image_total, HEADS * HD)
    projected = jnp.einsum(
        "nbc,cd->bnd", per_image, out_weight[0], preferred_element_type=jnp.float32
    )
    half_width = TEMB // 2
    frequency = jnp.exp(-math.log(10000.0) * jnp.arange(half_width, dtype=jnp.float32) / half_width)
    angles = timesteps[0].astype(jnp.float32)[:, None] * frequency
    features = jnp.concatenate([jnp.cos(angles), jnp.sin(angles)], axis=-1)
    activated = jax.nn.silu(features).astype(jnp.bfloat16)
    gate_share = jnp.dot(activated, gate_weight[0], preferred_element_type=jnp.float32)
    gate_vec = lax.all_gather(gate_share, "seq", axis=1, tiled=True)
    mixed = block_in.astype(jnp.float32) + gate_vec[:, None, :] * projected
    return mixed.astype(jnp.bfloat16)[None]


def solution(mesh):
    in_specs = (
        P("section", None, "seq", None),
        P(None, "seq", None),
        P("section", "seq", None),
        P("section", "seq", None),
        P("section", "seq", None),
        P("section", "seq", None),
        P("section", "seq", None),
        P(),
        P("section", None),
        P("section", None),
        P("section", None),
        P("section", None, None),
        P("section", None, "seq"),
    )
    out_specs = P("section", None, "seq", None)
    return jax.shard_map(local, mesh=mesh, in_specs=in_specs, out_specs=out_specs, check_vma=False)
```

profile of v0, /device:TPU:8, one launch (start us, length us, event | category | flops | bytes accessed | tf_op | source)
XLA Modules:
  0.0 504.2 jit_solution(978377741893471070)
XLA Ops:
  9.8 2.1 all_to_all.48
  12.5 1.6 reshape.178
  14.1 14.6 %all-to-all-start.1 = ((bf16[64,2,2048]{2,1,0:T(2,128)(2,1)}), bf16[64,2,2048]{2,1,0:T(2,128)(2,1)S(1)}, u32[]{:S(2)}, u32[]{:S(2)}) async-start(bf16[64,2,2048]{2,1,0:T(2,128)(2,1)} %reshape.178), calls=%async_computation.1 | async-start | bytes 1048576 | tf_op jit(solution)/shard_map/all_to_all | solution.py:76
  32.1 18.4 %all-to-all-done.1 = bf16[64,2,2048]{2,1,0:T(2,128)(2,1)S(1)} async-done(((bf16[64,2,2048]{2,1,0:T(2,128)(2,1)}), bf16[64,2,2048]{2,1,0:T(2,128)(2,1)S(1)}, u32[]{:S(2)}, u32[]{:S(2)}) %all-to-all-start.1) | async-done | bytes 524320 | tf_op jit(solution)/shard_map/all_to_all | solution.py:76
  50.4 5.7 %all-to-all-start = ((bf16[64,2,2048]{2,1,0:T(2,128)(2,1)}), bf16[64,2,2048]{2,1,0:T(2,128)(2,1)S(1)}, u32[]{:S(2)}, u32[]{:S(2)}) async-start(bf16[64,2,2048]{2,1,0:T(2,128)(2,1)} %reshape.176), calls=%async_computation | async-start | bytes 1048576 | tf_op jit(solution)/shard_map/all_to_all | solution.py:75
  59.5 23.0 %all-to-all-done = bf16[64,2,2048]{2,1,0:T(2,128)(2,1)S(1)} async-done(((bf16[64,2,2048]{2,1,0:T(2,128)(2,1)}), bf16[64,2,2048]{2,1,0:T(2,128)(2,1)S(1)}, u32[]{:S(2)}, u32[]{:S(2)}) %all-to-all-start) | async-done | bytes 524320 | tf_op jit(solution)/shard_map/all_to_all | solution.py:75
  82.6 6.4 %all-to-all-start.2 = ((bf16[64,2,2048]{2,1,0:T(2,128)(2,1)}), bf16[64,2,2048]{2,1,0:T(2,128)(2,1)}, u32[]{:S(2)}, u32[]{:S(2)}) async-start(bf16[64,2,2048]{2,1,0:T(2,128)(2,1)} %reshape.180), calls=%async_computation.2 | async-start | bytes 1048576 | tf_op jit(solution)/shard_map/all_to_all | solution.py:77
  93.1 19.3 %all-to-all-done.2 = bf16[64,2,2048]{2,1,0:T(2,128)(2,1)} async-done(((bf16[64,2,2048]{2,1,0:T(2,128)(2,1)}), bf16[64,2,2048]{2,1,0:T(2,128)(2,1)}, u32[]{:S(2)}, u32[]{:S(2)}) %all-to-all-start.2) | async-done | bytes 524320 | tf_op jit(solution)/shard_map/all_to_all | solution.py:77
  112.3 2.3 reshape.181
  117.2 17.9 %all-gather.6.cloned.1.call-done = bf16[1,384,4096]{2,0,1:T(2,128)(2,1)} async-done(((bf16[1,6,4096]{2,0,1:T(2,128)(2,1)}), bf16[1,384,4096]{2,0,1:T(2,128)(2,1)}) %all-gather.6.cloned.1.call-update) | async-done | bytes 3145744 | tf_op jit(solution)/shard_map/all_gather | solution.py:80
  136.8 101.4 %all-gather.8.cloned.1.call-done = bf16[1,384,4096]{2,0,1:T(2,128)(2,1)} async-done(((bf16[1,6,4096]{2,0,1:T(2,128)(2,1)}), bf16[1,384,4096]{2,0,1:T(2,128)(2,1)}) %all-gather.8.cloned.1.call-update) | async-done | bytes 3145744 | tf_op jit(solution)/shard_map/all_gather | solution.py:81
  239.5 1.9 pad_maximum_fusion
  241.3 41.0 %while.18 = (s32[]{:T(128)}, bf16[8,512,64]{1,2,0:T(8,128)(2,1)S(1)}, bf16[8,512,64]{2,1,0:T(8,128)(2,1)}, bf16[4480,64]{1,0:T(8,128)(2,1)}, bf16[4480,64]{1,0:T(8,128)(2,1)}, /*index=5*/s32[]{:T(128)}, s32[]{:T(128)}) while((s32[]{:T(128)}, bf16[8,512,64]{1,2,0:T(8,128)(2,1)S(1)}, bf16[8,512,64]{2,1,0:T(8,128)(2,1)}, ...), condition=%wide.region_5.6_spmd.clone, body=%wide.region_3.5_spmd.clone.sunk | while | flops 598708096 | bytes 23147888 | solution.py:40
  241.4 3.4 fusion.39
  244.8 1.6 fusion.40
  246.5 3.4 fusion.39
  249.9 1.6 fusion.40
  251.6 3.4 fusion.39
  255.1 1.6 fusion.40
  256.7 3.4 fusion.39
  260.2 1.6 fusion.40
  261.9 3.4 fusion.39
  265.3 1.6 fusion.40
  267.0 3.4 fusion.39
  270.4 1.6 fusion.40
  272.1 3.4 fusion.39
  275.6 1.6 fusion.40
  277.3 3.4 fusion.39
  280.7 1.6 fusion.40
  285.5 10.6 %all-to-all-start.3 = ((bf16[64,2,2048]{2,1,0:T(2,128)(2,1)}), bf16[64,2,2048]{2,1,0:T(2,128)(2,1)S(1)}, u32[]{:S(2)}, u32[]{:S(2)}) async-start(bf16[64,2,2048]{2,1,0:T(2,128)(2,1)} %reshape.182), calls=%async_computation.3 | async-start | bytes 1048576 | tf_op jit(solution)/shard_map/all_to_all | solution.py:100
  297.7 192.4 %all-gather.2 = f32[64,38,2]{1,2,0:T(2,128)S(1)} all-gather(f32[1,38,2]{1,2,0:T(2,128)S(1)} %convolution_bitcast_fusion), channel_id=1, replica_groups=mesh['section'=4,'seq'=64] {'seq'}, dimensions={0}, use_global_device_ids=true | all-gather | bytes 19760 | tf_op jit(solution)/shard_map/all_gather | solution.py:111
  491.0 6.3 %fusion.20 = bf16[1,2,64,2432]{3,2,1,0:T(8,128)(2,1)} fusion(bf16[1,2,64,2432]{3,2,1,0:T(8,128)(2,1)S(1)} %collective-permute-done, bf16[2,64,2432]{2,1,0:T(8,128)(2,1)S(1)} %copy-done.2, bf16[64,2,2048]{0,2,1:T(8,128)(2,1)S(1)} %bitcast.107, bf16[1,2048,2432]{2,1,0:T(8,128)(2,1)} %param.26, f32[2,2432]{1,0:T(2,128)S(1)} %bitcast.116, pred[]{:T(512)S(6)} %eq.3), kind=kOutput, calls=%fused_computation.26 | convolution fusion | flops 1276624896 | bytes 12372993 | tf_op jit(solution)/shard_map/nbc,cd->bnd/dot_general | solution.py:102
  (90 shorter events, 25.0 us)
Async XLA Ops:
  6.5 291.0 %copy-start = (bf16[1,256,38]{1,2,0:T(8,128)(2,1)S(1)}, bf16[1,256,38]{1,2,0:T(8,128)(2,1)}, u32[]{:S(2)}) copy-start(bf16[1,256,38]{1,2,0:T(8,128)(2,1)} %param.27) | copy-start | bytes 58372
  6.5 128.6 %all-gather.6.cloned.1.call-start = ((), (), s32[]{:S(2)}) async-start(), calls=%async_computation.4 | async-start | bytes 6389760 | tf_op jit(solution)/shard_map/all_gather | solution.py:80
  8.1 230.1 %all-gather.8.cloned.1.call-start = ((), (), s32[]{:S(2)}) async-start(), calls=%async_computation.5 | async-start | bytes 6389760 | tf_op jit(solution)/shard_map/all_gather | solution.py:81
  11.8 16.9 %copy-start.3 = (bf16[1,64,4096]{2,1,0:T(8,128)(2,1)S(1)}, bf16[1,64,4096]{2,1,0:T(8,128)(2,1)}, u32[]{:S(2)}) copy-start(bf16[1,64,4096]{2,1,0:T(8,128)(2,1)} %param.17) | copy-start | bytes 1572868
  14.1 36.3 %all-to-all-start.1 = ((bf16[64,2,2048]{2,1,0:T(2,128)(2,1)}), bf16[64,2,2048]{2,1,0:T(2,128)(2,1)S(1)}, u32[]{:S(2)}, u32[]{:S(2)}) async-start(bf16[64,2,2048]{2,1,0:T(2,128)(2,1)} %reshape.178), calls=%async_computation.1 | async-start | bytes 1048576 | tf_op jit(solution)/shard_map/all_to_all | solution.py:76
  30.5 25.6 %copy-start.4 = (bf16[1,64,4096]{2,1,0:T(8,128)(2,1)S(1)}, bf16[1,64,4096]{2,1,0:T(8,128)(2,1)}, u32[]{:S(2)}) copy-start(bf16[1,64,4096]{2,1,0:T(8,128)(2,1)} %param.19) | copy-start | bytes 1572868
  50.4 32.1 %all-to-all-start = ((bf16[64,2,2048]{2,1,0:T(2,128)(2,1)}), bf16[64,2,2048]{2,1,0:T(2,128)(2,1)S(1)}, u32[]{:S(2)}, u32[]{:S(2)}) async-start(bf16[64,2,2048]{2,1,0:T(2,128)(2,1)} %reshape.176), calls=%async_computation | async-start | bytes 1048576 | tf_op jit(solution)/shard_map/all_to_all | solution.py:75
  57.3 31.7 %copy-start.9 = (s32[2]{0:T(128)S(1)}, s32[2]{0:T(128)}, u32[]{:S(2)}) copy-start(s32[2]{0:T(128)} %param.22) | copy-start | bytes 28
  82.6 29.8 %all-to-all-start.2 = ((bf16[64,2,2048]{2,1,0:T(2,128)(2,1)}), bf16[64,2,2048]{2,1,0:T(2,128)(2,1)}, u32[]{:S(2)}, u32[]{:S(2)}) async-start(bf16[64,2,2048]{2,1,0:T(2,128)(2,1)} %reshape.180), calls=%async_computation.2 | async-start | bytes 1048576 | tf_op jit(solution)/shard_map/all_to_all | solution.py:77
  93.1 21.9 %copy-start.7 = (f32[1,64]{1,0:T(1,128)S(1)}, f32[1,64]{1,0:T(1,128)}, u32[]{:S(2)}) copy-start(f32[1,64]{1,0:T(1,128)} %param.24) | copy-start | bytes 772
  114.9 1.6 copy-start.6
  239.5 1.9 copy-start.5
  241.4 3.4 copy-start.1
  246.5 3.4 copy-start.1
  251.6 3.4 copy-start.1
  256.7 3.4 copy-start.1
  261.9 3.4 copy-start.1
  267.0 3.4 copy-start.1
  272.1 3.4 copy-start.1
  277.3 3.4 copy-start.1
  283.2 12.9 %copy-start.8 = (bf16[1,2,64,2432]{3,2,1,0:T(8,128)(2,1)S(1)}, bf16[1,2,64,2432]{3,2,1,0:T(8,128)(2,1)}, u32[]{:S(2)}) copy-start(bf16[1,2,64,2432]{3,2,1,0:T(8,128)(2,1)} %param.15) | copy-start | bytes 1867780
  283.2 14.2 %copy-start.10 = (s32[1,2]{1,0:T(1,128)S(1)}, s32[1,2]{1,0:T(1,128)}, u32[]{:S(2)}) copy-start(s32[1,2]{1,0:T(1,128)} %param.23) | copy-start | bytes 28
  283.9 207.1 %copy-start.2 = (bf16[2,64,2432]{2,1,0:T(8,128)(2,1)S(1)}, bf16[2,64,2432]{2,1,0:T(8,128)(2,1)}, u32[]{:S(2)}) copy-start(bf16[2,64,2432]{2,1,0:T(8,128)(2,1)} %param.16) | copy-start | bytes 1867780
  285.5 204.8 %all-to-all-start.3 = ((bf16[64,2,2048]{2,1,0:T(2,128)(2,1)}), bf16[64,2,2048]{2,1,0:T(2,128)(2,1)S(1)}, u32[]{:S(2)}, u32[]{:S(2)}) async-start(bf16[64,2,2048]{2,1,0:T(2,128)(2,1)} %reshape.182), calls=%async_computation.3 | async-start | bytes 1048576 | tf_op jit(solution)/shard_map/all_to_all | solution.py:100
  296.1 194.9 %collective-permute-start = (bf16[1,2,64,2432]{3,2,1,0:T(8,128)(2,1)S(1)}, bf16[1,2,64,2432]{3,2,1,0:T(8,128)(2,1)S(1)}, u32[]{:S(2)}, u32[]{:S(2)}) collective-permute-start(bf16[1,2,64,2432]{3,2,1,0:T(8,128)(2,1)S(1)} %copy-done.8), channel_id=1, source_target_pairs={{0,64},{64,128},{128,192},{1,65},{65,129},{129,193},{2,66},{66,130... | collective-permute-start | bytes 1867784 | tf_op jit(solution)/shard_map/ppermute | solution.py:16
Sparse Core Ops, SparseCore 0:
  10.6 124.4 all-gather.5
  138.4 99.7 all-gather.7
where the time goes:
time: 505 us; the launch traced here: 504 us
  blocking collectives  192 us (38%)
  waiting for transfers between devices  180 us (36%)
  matrix products  47 us (9%)
  starting transfers between devices  38.6 us (8%)
  local copies, waits for them, and re-layouts  23.8 us (5%)
  between operations  14.4 us (3%)
  other arithmetic  7.49 us (1%)
    all_gather x1, blocking collectives, local(): gate_vec = lax.all_gather(gate_share, 'seq', axis=1, tiled=True)  192 us
    all_gather x1, waiting for transfers between devices, local(): lax.all_gather(local_text_value, 'seq', axis=0, tiled=True)  101 us
    dot_general x8, matrix products, one_block(): jnp.einsum('qd,kd->qk', query_block, key_rows, preferred_element_type=jnp...  27.5 us
    all_to_all x1, waiting for transfers between devices, local(): lax.all_to_all(local_query, 'seq', split_axis=1, concat_axis=0, tiled=True)  23 us
    all_to_all x1, waiting for transfers between devices, local(): lax.all_to_all(local_value, 'seq', split_axis=1, concat_axis=0, tiled=True)  19.3 us
    all_to_all x1, waiting for transfers between devices, local(): lax.all_to_all(local_key, 'seq', split_axis=1, concat_axis=0, tiled=True)  18.4 us
    all_gather x1, waiting for transfers between devices, local(): lax.all_gather(local_text_key, 'seq', axis=0, tiled=True)  17.9 us
    all_to_all x1, starting transfers between devices, local(): lax.all_to_all(local_key, 'seq', split_axis=1, concat_axis=0, tiled=True)  14.6 us
  transfers between devices with their start and end apart: 7, of which 5 were waited for; matrix products, arithmetic and copies ran while one was open for 4% of the time, Pallas kernels for 0%

commit v1 on v0

v1 whole, which is shorter than its diff:
```python
import functools
import math

import jax
import jax.numpy as jnp
from jax import lax
from jax.experimental import pallas as pl
from jax.experimental.pallas import tpu as pltpu
from jax.sharding import PartitionSpec as P

MESH = pl.DeviceIdType.MESH
HD = 64
LANES = 128
TEMB = 256
TEXT_SLOT = 8
SCALE = math.log2(math.e) / math.sqrt(HD)
F32 = jnp.float32
BF16 = jnp.bfloat16


def lanes_below_half(shape):
    return lax.broadcasted_iota(jnp.int32, shape, len(shape) - 1) < HD


def swap_halves(data):
    return pltpu.roll(data, HD, len(data.shape) - 1)


def normed(data, gain):
    squares = data * data
    high = squares.astype(BF16)
    low = (squares - high.astype(F32)).astype(BF16)
    row = lax.broadcasted_iota(jnp.int32, (LANES, LANES), 0) // HD
    col = lax.broadcasted_iota(jnp.int32, (LANES, LANES), 1) // HD
    halves = jnp.where(row == col, 1.0, 0.0).astype(BF16)
    total = jnp.dot(high, halves, preferred_element_type=F32)
    total = total + jnp.dot(low, halves, preferred_element_type=F32)
    return data * lax.rsqrt(total * (1.0 / HD) + 1e-6) * gain


def kernel(
    seq_count,
    group_slots,
    key_tile,
    counts,
    times,
    queries,
    keys,
    values,
    text_keys,
    text_values,
    query_gain,
    key_gain,
    gate_weight,
    out_weight,
    stale,
    fresh,
    out,
    kv_send,
    kv_recv,
    q_send,
    q_recv,
    o_send,
    o_recv,
    text_pad,
    text_k,
    value_aug,
    gate_pad,
    gate_acc,
    weight,
    block_in,
    lhs,
    kv_send_sem,
    kv_recv_sem,
    q_send_sem,
    q_recv_sem,
    o_send_sem,
    o_recv_sem,
    weight_sem,
    shift_send_sem,
    shift_recv_sem,
):
    me = lax.axis_index("seq")
    section = lax.axis_index("section")
    sections = lax.axis_size("section")
    rows = queries.shape[0]
    half = rows // 2
    text_rows = text_keys.shape[0]
    pair_count = seq_count // 2
    gate_span = gate_weight.shape[1]
    groups = seq_count // group_slots
    image_items = seq_count // 2

    barrier = pltpu.get_barrier_semaphore()

    def greet(step, carry):
        pl.semaphore_signal(
            barrier, inc=1, device_id={"seq": lax.rem(me + step, seq_count)}, device_id_type=MESH
        )
        return carry

    lax.fori_loop(1, seq_count, greet, 0)

    @pl.when(section > 0)
    def _():
        pl.semaphore_signal(barrier, inc=1, device_id={"section": section - 1}, device_id_type=MESH)

    load_weight = pltpu.make_async_copy(out_weight, weight, weight_sem)
    load_weight.start()

    text_pad[...] = jnp.zeros_like(text_pad)
    text_pad[0, 0:text_rows, :] = text_keys[...].astype(F32)
    text_pad[1, 0:text_rows, :] = text_values[...].astype(F32)

    row8 = lax.broadcasted_iota(jnp.int32, (8, LANES), 0)
    lane8 = lax.broadcasted_iota(jnp.int32, (8, LANES), 1)
    stamp = jnp.where(row8 % 2 == 0, times[0], times[1]).astype(F32)
    angles = stamp * jnp.exp(lane8.astype(F32) * (-math.log(10000.0) / (TEMB // 2)))
    features = jnp.concatenate([jnp.cos(angles), jnp.sin(angles)], axis=1)
    activated = (features / (1.0 + jnp.exp(-features))).astype(BF16)
    gate_pad[...] = jnp.zeros_like(gate_pad)
    gate_pad[:, 0:gate_span] = jnp.dot(activated, gate_weight[...], preferred_element_type=F32)
    gate_row = pltpu.roll(gate_pad[...], lax.rem(me * gate_span, LANES), 1)
    gate_high = gate_row.astype(BF16).astype(F32)
    gate_low = gate_row - gate_high
    gate_rows = jnp.where(
        row8 < 2,
        gate_high[:, :LANES],
        jnp.where(
            row8 < 4, gate_low[:, :LANES], jnp.where(row8 < 6, gate_high[:, LANES:], gate_low[:, LANES:])
        ),
    )

    @pl.when(section < sections - 1)
    def _():
        pl.semaphore_wait(barrier, seq_count)

    @pl.when(section == sections - 1)
    def _():
        pl.semaphore_wait(barrier, seq_count - 1)

    def send_kv(target, chunk, text_chunk):
        slot = kv_send.at[target]
        slot[0:rows, :] = chunk
        slot[rows:, :] = text_chunk

        @pl.when(target != me)
        def _():
            pltpu.make_async_remote_copy(
                slot, kv_recv.at[me], kv_send_sem, kv_recv_sem, device_id={"seq": target}, device_id_type=MESH
            ).start()

        @pl.when(target == me)
        def _():
            kv_recv[me, 0:rows, :] = chunk
            kv_recv[me, rows:, :] = text_chunk

    def pack_kv(step, carry):
        pair = lax.rem(me // 2 + step, pair_count)
        columns = pl.ds(pl.multiple_of(pair * LANES, LANES), LANES)
        gain = key_gain[...]
        key = normed(keys[:, columns].astype(F32), gain).astype(BF16)
        value = values[:, columns]
        below = lanes_below_half((rows, LANES))
        text_key = normed(text_pad[0, :, columns], gain)
        text_value = text_pad[1, :, columns]
        below8 = lanes_below_half((TEXT_SLOT, LANES))
        first = jnp.where(below, key, swap_halves(value))
        second = jnp.where(below, swap_halves(key), value)
        text_first = jnp.where(below8, text_key, swap_halves(text_value))
        text_second = jnp.where(below8, swap_halves(text_key), text_value)
        send_kv(2 * pair, first, jnp.concatenate([text_first, gate_rows], axis=0).astype(BF16))
        send_kv(2 * pair + 1, second, jnp.concatenate([text_second, gate_rows], axis=0).astype(BF16))
        return carry

    lax.fori_loop(0, pair_count, pack_kv, 0)

    def send_q(target, chunk):
        ahead = lax.rem(target - me + seq_count, seq_count)

        @pl.when(target != me)
        def _():
            q_send[ahead] = chunk
            pltpu.make_async_remote_copy(
                q_send.at[ahead],
                q_recv.at[ahead],
                q_send_sem,
                q_recv_sem.at[ahead // group_slots],
                device_id={"seq": target},
                device_id_type=MESH,
            ).start()

        @pl.when(target == me)
        def _():
            q_recv[0] = chunk

    def pack_q(step, carry):
        pair = lax.rem(me // 2 + step, pair_count)
        columns = pl.ds(pl.multiple_of(pair * LANES, LANES), LANES)
        data = normed(queries[:, columns].astype(F32), query_gain[...]).astype(BF16)
        below = lanes_below_half((half, LANES))
        top, bottom = data[0:half], data[half:]
        send_q(2 * pair, jnp.where(below, top, swap_halves(bottom)))
        send_q(2 * pair + 1, jnp.where(below, swap_halves(top), bottom))
        return carry

    lax.fori_loop(0, pair_count, pack_q, 0)

    @pl.when(section == 0)
    def _():
        pltpu.make_async_copy(fresh, block_in, shift_recv_sem).start()

    shift = pltpu.make_async_remote_copy(
        stale,
        block_in,
        shift_send_sem,
        shift_recv_sem,
        device_id={"section": lax.rem(section + 1, sections)},
        device_id_type=MESH,
    )

    @pl.when(section < sections - 1)
    def _():
        shift.start()

    others = pl.ds(0, seq_count - 1)

    def all_others(send, recv, send_sem, recv_sem):
        return pltpu.make_async_remote_copy(
            send.at[others],
            recv.at[others],
            send_sem,
            recv_sem,
            device_id={"seq": lax.rem(me + 1, seq_count)},
            device_id_type=MESH,
        )

    all_others(kv_send, kv_recv, kv_send_sem, kv_recv_sem).wait_recv()

    live_count = counts[me // image_items]

    def augment(step, carry):
        block = kv_recv[step]
        below = lanes_below_half((rows, LANES))
        value_aug[pl.ds(pl.multiple_of(step * rows, rows), rows), :] = jnp.where(
            below, jnp.ones((), BF16), block[0:rows]
        )
        return carry

    lax.fori_loop(0, seq_count, augment, 0)
    text_total = seq_count * TEXT_SLOT
    image_total = seq_count * rows
    text_all = kv_recv[:, rows : rows + 16, :].astype(F32)[:, 0:TEXT_SLOT, :].reshape(text_total, LANES)
    text_k[...] = text_all.astype(BF16)
    place = lax.broadcasted_iota(jnp.int32, (text_total, LANES), 0)
    within = place % TEXT_SLOT
    live = (within < text_rows) & ((place // TEXT_SLOT) * text_rows + within < live_count)
    value_aug[image_total:, :] = jnp.where(
        live, jnp.where(lanes_below_half((text_total, LANES)), 1.0, text_all), 0.0
    ).astype(BF16)

    gate_acc[...] = jnp.zeros_like(gate_acc)

    def collect_gate(step, carry):
        tile = (step * gate_span) // LANES
        columns = pl.ds(pl.multiple_of(tile * LANES, LANES), LANES)
        gate_acc[:, columns] = gate_acc[:, columns] + kv_recv[step, rows : rows + 16, :].astype(F32)[8:16]
        return carry

    lax.fori_loop(0, seq_count, collect_gate, 0)

    key_blocks = key_tile // rows
    tiles = [(start, key_tile) for start in range(0, image_total, key_tile)]
    tiles += [(image_total + start, min(key_tile, text_total)) for start in range(0, text_total, key_tile)]

    def attend(group, carry):
        first_slot = pl.multiple_of(group * group_slots, group_slots)

        @pl.when(group == 0)
        def _():
            pltpu.make_async_copy(
                q_recv.at[pl.ds(0, group_slots - 1)], q_recv.at[pl.ds(0, group_slots - 1)], q_recv_sem.at[0]
            ).wait()

        @pl.when(group > 0)
        def _():
            pltpu.make_async_copy(
                q_recv.at[pl.ds(0, group_slots)], q_recv.at[pl.ds(0, group_slots)], q_recv_sem.at[group]
            ).wait()

        packed = q_recv[pl.ds(first_slot, group_slots)].reshape(group_slots * half, LANES)
        below = lanes_below_half(packed.shape)
        zero = jnp.zeros((), BF16)
        query = jnp.concatenate(
            [jnp.where(below, packed, zero), jnp.where(below, swap_halves(packed), zero)], axis=0
        )
        total = jnp.zeros((group_slots * rows, LANES), F32)
        for start, size in tiles:
            if start < image_total:
                key = kv_recv[start // rows : (start + size) // rows, 0:rows, :].reshape(size, LANES)
            else:
                key = text_k[start - image_total : start - image_total + size, :]
            scores = lax.dot_general(query, key, (((1,), (1,)), ((), ())), preferred_element_type=F32)
            weights = jnp.exp2(scores * SCALE).astype(BF16)
            total = total + jnp.dot(weights, value_aug[start : start + size, :], preferred_element_type=F32)
        result = total / swap_halves(total)
        top, bottom = result[0 : group_slots * half], result[group_slots * half :]
        mixed = jnp.where(below, swap_halves(top), bottom).astype(BF16)
        o_send[pl.ds(first_slot, group_slots)] = mixed.reshape(group_slots, half, LANES)

        def send_back(step, inner):
            ahead = first_slot + step

            @pl.when(ahead > 0)
            def _():
                pltpu.make_async_remote_copy(
                    o_send.at[ahead],
                    o_recv.at[me],
                    o_send_sem,
                    o_recv_sem,
                    device_id={"seq": lax.rem(me - ahead + seq_count, seq_count)},
                    device_id_type=MESH,
                ).start()

            return inner

        lax.fori_loop(0, group_slots, send_back, 0)
        return carry

    lax.fori_loop(0, groups, attend, 0)
    o_recv[me] = o_send[0]

    load_weight.wait()

    @pl.when(section == 0)
    def _():
        pltpu.make_async_copy(fresh, block_in, shift_recv_sem).wait()

    @pl.when(section > 0)
    def _():
        shift.wait_recv()

    gate_sum = gate_acc[...]
    ahead_tile = gate_sum[4:8, : out.shape[2]]
    gate_first = gate_sum[0:4, : out.shape[2]]
    gate_next = jnp.concatenate([jnp.zeros((4, LANES), F32), ahead_tile[:, : out.shape[2] - LANES]], axis=1)
    gate_four = gate_first + gate_next
    gate_vec = gate_four[0:2] + gate_four[2:4]

    all_others(o_send, o_recv, o_send_sem, o_recv_sem).wait_recv()

    below_half = lanes_below_half((half, LANES))
    for image in range(2):
        for pair in range(image_items // 2):
            one, two = o_recv[image * image_items + 2 * pair], o_recv[image * image_items + 2 * pair + 1]
            columns = slice(pair * LANES, (pair + 1) * LANES)
            lhs[image * rows : image * rows + half, columns] = jnp.where(below_half, one, swap_halves(two))
            lhs[image * rows + half : (image + 1) * rows, columns] = jnp.where(below_half, swap_halves(one), two)

    width = out.shape[2]
    attended = lhs[...]
    for start in range(0, width, 512):
        stop = min(start + 512, width)
        projected = jnp.dot(attended, weight[:, start:stop], preferred_element_type=F32)
        for image in range(2):
            part = projected[image * rows : (image + 1) * rows]
            held = block_in[image, :, start:stop].astype(F32)
            out[image, :, start:stop] = (held + gate_vec[image : image + 1, start:stop] * part).astype(BF16)

    all_others(kv_send, kv_recv, kv_send_sem, kv_recv_sem).wait_send()
    all_others(q_send, q_recv, q_send_sem, q_recv_sem.at[0]).wait_send()
    all_others(o_send, o_recv, o_send_sem, o_recv_sem).wait_send()

    @pl.when(section < sections - 1)
    def _():
        shift.wait_send()


def solution(mesh):
    seq_count = mesh.shape["seq"]
    group_slots = 8
    key_tile = 512

    def step(
        stale,
        fresh,
        queries,
        image_keys,
        image_values,
        text_keys,
        text_values,
        text_count,
        timesteps,
        query_gain,
        key_gain,
        out_weight,
        gate_weight,
    ):
        images, rows, width = fresh.shape
        half = rows // 2
        message = rows + 2 * TEXT_SLOT
        columns = queries.shape[2]
        padded = -(-width // LANES) * LANES + LANES
        vmem = pl.BlockSpec(memory_space=pltpu.VMEM)
        smem = pl.BlockSpec(memory_space=pltpu.SMEM)
        hbm = pl.BlockSpec(memory_space=pl.ANY)
        result = pl.pallas_call(
            functools.partial(kernel, seq_count, group_slots, key_tile),
            out_shape=jax.ShapeDtypeStruct((images, rows, width), BF16),
            in_specs=[smem, smem] + [vmem] * 8 + [hbm] * 3,
            out_specs=vmem,
            scratch_shapes=[
                pltpu.VMEM((seq_count, message, LANES), BF16),
                pltpu.VMEM((seq_count, message, LANES), BF16),
                pltpu.VMEM((seq_count, half, LANES), BF16),
                pltpu.VMEM((seq_count, half, LANES), BF16),
                pltpu.VMEM((seq_count, half, LANES), BF16),
                pltpu.VMEM((seq_count, half, LANES), BF16),
                pltpu.VMEM((2, TEXT_SLOT, columns), F32),
                pltpu.VMEM((seq_count * TEXT_SLOT, LANES), BF16),
                pltpu.VMEM((seq_count * (rows + TEXT_SLOT), LANES), BF16),
                pltpu.VMEM((8, 2 * LANES), F32),
                pltpu.VMEM((8, padded), F32),
                pltpu.VMEM(out_weight.shape[1:], BF16),
                pltpu.VMEM((images, rows, width), BF16),
                pltpu.VMEM((images * rows, out_weight.shape[1]), BF16),
                pltpu.SemaphoreType.DMA,
                pltpu.SemaphoreType.DMA,
                pltpu.SemaphoreType.DMA,
                pltpu.SemaphoreType.DMA((seq_count // group_slots,)),
                pltpu.SemaphoreType.DMA,
                pltpu.SemaphoreType.DMA,
                pltpu.SemaphoreType.DMA,
                pltpu.SemaphoreType.DMA,
                pltpu.SemaphoreType.DMA,
            ],
            compiler_params=pltpu.CompilerParams(
                collective_id=0, has_side_effects=True, vmem_limit_bytes=56 * 1024 * 1024
            ),
            name="joint_attention",
        )(
            text_count,
            timesteps[0],
            queries[0],
            image_keys[0],
            image_values[0],
            text_keys[0],
            text_values[0],
            jnp.tile(query_gain, (1, 2)),
            jnp.tile(key_gain, (1, 2)),
            gate_weight[0],
            out_weight[0],
            stale[0],
            fresh,
        )
        return result[None]

    return jax.shard_map(
        step,
        mesh=mesh,
        in_specs=(
            P("section", None, "seq", None),
            P(None, "seq", None),
            P("section", "seq", None),
            P("section", "seq", None),
            P("section", "seq", None),
            P("section", "seq", None),
            P("section", "seq", None),
            P(),
            P("section", None),
            P("section", None),
            P("section", None),
            P("section", None, None),
            P("section", None, "seq"),
        ),
        out_specs=P("section", None, "seq", None),
        check_vma=False,
    )
```

time: 505 us -> 102 us (0.20)
  the two profiles are of different devices: /device:TPU:8 before, /device:TPU:1 now
where the time goes in v1:
time: 102 us
  Pallas kernels  96.1 us (94%)
  local copies, waits for them, and re-layouts  5.97 us (6%)
    pallas_call x1, Pallas kernels, step(): pl.pallas_call(functools.partial(kernel, seq_count, group_slots, key_tile...  96.1 us
    unnamed x2, local copies, waits for them, and re-layouts  3.42 us

profile of v1, /device:TPU:1, one launch (start us, length us, event | category | flops | bytes accessed | tf_op | source)
XLA Modules:
  0.0 102.1 jit_solution(14802286801207294226)
XLA Ops:
  0.0 0.7 tile.23
  0.7 0.7 tile.24.query_gain
  1.3 0.7 tile.26
  2.0 0.6 tile.27.key_gain
  2.6 1.5 %copy.14 = bf16[1,256,38]{2,1,0:T(8,128)(2,1)} copy(bf16[1,256,38]{1,2,0:T(8,128)(2,1)} %param.25) | data formatting | bytes 38912 | tf_op args[12]
  4.0 96.1 %joint_attention.1 = bf16[2,64,2432]{2,1,0:T(8,128)(2,1)} custom-call(s32[2]{0:T(128)} %counts.1, s32[2]{0:T(128)} %bitcast.21, bf16[64,4096]{1,0:T(8,128)(2,1)} %bitcast.15, bf16[64,4096]{1,0:T(8,128)(2,1)} %bitcast.16, bf16[64,4096]{1,0:T(8,128)(2,1)} %bitcast.17, bf16[6,4096]{1,0:T(8,128)(2,1)} %bitcast.19, bf16[6,4096]{1,0:T(8,128)(2,1)} %bitcast.20, ...), custom_call_target="tpu_custom_call" | custom-call | tf_op jit(solution)/shard_map/joint_attention/pallas_call | solution.py:407
  100.2 1.9 %copy.16 = bf16[1,2,64,2432]{3,2,1,0:T(8,128)(2,1)} copy(bf16[1,2,64,2432]{3,2,1,0:T(8,128)(2,1)} %bitcast.13) | data formatting | bytes 1245184

commit v2 on v1

v2 whole, which is shorter than its diff:
```python
import functools
import math

import jax
import jax.numpy as jnp
from jax import lax
from jax.experimental import pallas as pl
from jax.experimental.pallas import tpu as pltpu
from jax.sharding import PartitionSpec as P

MESH = pl.DeviceIdType.MESH
HD = 64
LANES = 128
TEMB = 256
TEXT_SLOT = 8
SCALE = math.log2(math.e) / math.sqrt(HD)
F32 = jnp.float32
BF16 = jnp.bfloat16


def lanes_below_half(shape):
    return lax.broadcasted_iota(jnp.int32, shape, len(shape) - 1) < HD


def swap_halves(data):
    return pltpu.roll(data, HD, len(data.shape) - 1)


def normed(parts, gain):
    data = jnp.concatenate(parts, axis=0)
    squares = data * data
    high = squares.astype(BF16)
    low = (squares - high.astype(F32)).astype(BF16)
    row = lax.broadcasted_iota(jnp.int32, (2 * LANES, LANES), 0) // HD
    col = lax.broadcasted_iota(jnp.int32, (2 * LANES, LANES), 1) // HD
    halves = jnp.where(row % 2 == col, 1.0, 0.0).astype(BF16)
    total = jnp.dot(jnp.concatenate([high, low], axis=1), halves, preferred_element_type=F32)
    data = data * lax.rsqrt(total * (1.0 / HD) + 1e-6) * gain
    sizes = [part.shape[0] for part in parts]
    return [data[sum(sizes[:at]) : sum(sizes[: at + 1])] for at in range(len(parts))]


def kernel(
    seq_count,
    span,
    counts,
    times,
    text_keys,
    text_values,
    query_gain,
    key_gain,
    gate_weight,
    queries_hbm,
    keys_hbm,
    values_hbm,
    out_weight,
    stale,
    fresh,
    out,
    queries,
    keys,
    values,
    text_send,
    text_recv,
    q_send,
    q_recv,
    kv_send,
    kv_recv,
    o_send,
    o_recv,
    text_pad,
    text_k,
    text_v,
    value_aug,
    query_rows,
    total,
    gate_pad,
    gate_acc,
    weight,
    block_in,
    projected,
    load_sem,
    text_send_sem,
    text_recv_sem,
    q_send_sem,
    q_recv_sem,
    kv_send_sem,
    kv_recv_sem,
    o_send_sem,
    o_recv_sem,
    shift_send_sem,
    shift_recv_sem,
):
    me = lax.axis_index("seq")
    section = lax.axis_index("section")
    sections = lax.axis_size("section")
    rows = queries.shape[0]
    half = rows // 2
    text_rows = text_keys.shape[0]
    blocks = seq_count // span
    my_block, my_place = me // span, lax.rem(me, span)
    pairs = range(span // 2)
    block_rows = span * rows
    block_columns = span * HD
    gate_span = gate_weight.shape[0]
    width = out.shape[2]
    text_total = seq_count * TEXT_SLOT

    barrier = pltpu.get_barrier_semaphore()

    def greet(step, carry):
        pl.semaphore_signal(
            barrier, inc=1, device_id={"seq": lax.rem(me + step, seq_count)}, device_id_type=MESH
        )
        return carry

    lax.fori_loop(1, seq_count, greet, 0)

    @pl.when(section > 0)
    def _():
        pl.semaphore_signal(barrier, inc=1, device_id={"section": section - 1}, device_id_type=MESH)

    loads = [
        pltpu.make_async_copy(queries_hbm, queries, load_sem.at[0]),
        pltpu.make_async_copy(keys_hbm, keys, load_sem.at[1]),
        pltpu.make_async_copy(values_hbm, values, load_sem.at[2]),
        pltpu.make_async_copy(out_weight, weight, load_sem.at[3]),
    ]
    for load in loads:
        load.start()

    text_pad[...] = jnp.zeros_like(text_pad)
    text_pad[0, 0:text_rows, :] = text_keys[...].astype(F32)
    text_pad[1, 0:text_rows, :] = text_values[...].astype(F32)
    query_gain_both = jnp.concatenate([query_gain[...]] * 2, axis=1)
    key_gain_both = jnp.concatenate([key_gain[...]] * 2, axis=1)

    row8 = lax.broadcasted_iota(jnp.int32, (8, LANES), 0)
    lane8 = lax.broadcasted_iota(jnp.int32, (8, LANES), 1)
    stamp = jnp.where(row8 % 2 == 0, times[0], times[1]).astype(F32)
    angles = stamp * jnp.exp(lane8.astype(F32) * (-math.log(10000.0) / (TEMB // 2)))
    features = jnp.concatenate([jnp.cos(angles), jnp.sin(angles)], axis=1)
    activated = (features / (1.0 + jnp.exp(-features))).astype(BF16)
    gate_pad[...] = jnp.zeros_like(gate_pad)
    gate_pad[:, 0:gate_span] = lax.dot_general(
        activated, gate_weight[...], (((1,), (1,)), ((), ())), preferred_element_type=F32
    )
    gate_row = pltpu.roll(gate_pad[...], lax.rem(me * gate_span, LANES), 1)
    gate_high = gate_row.astype(BF16).astype(F32)
    gate_low = gate_row - gate_high
    gate_rows = jnp.where(
        row8 < 2,
        gate_high[:, :LANES],
        jnp.where(
            row8 < 4, gate_low[:, :LANES], jnp.where(row8 < 6, gate_high[:, LANES:], gate_low[:, LANES:])
        ),
    )

    below = lanes_below_half((rows, LANES))
    below8 = lanes_below_half((TEXT_SLOT, LANES))
    below_half = lanes_below_half((half, LANES))

    def tile(first, at):
        return pl.ds(pl.multiple_of(first * HD + at * LANES, LANES), LANES)

    def push(send, recv, send_sem, recv_sem, target):
        pltpu.make_async_remote_copy(
            send, recv, send_sem, recv_sem, device_id={"seq": target}, device_id_type=MESH
        ).start()

    def pack_text(step, carry):
        first = step * span
        normed_keys = normed([text_pad[0, :, tile(first, at)] for at in pairs], key_gain_both)
        for at, text_key in zip(pairs, normed_keys):
            text_value = text_pad[1, :, tile(first, at)]
            one = jnp.where(below8, text_key, swap_halves(text_value))
            two = jnp.where(below8, swap_halves(text_key), text_value)
            text_send[first + 2 * at] = jnp.concatenate([one, gate_rows], axis=0).astype(BF16)
            text_send[first + 2 * at + 1] = jnp.concatenate([two, gate_rows], axis=0).astype(BF16)
        return carry

    lax.fori_loop(0, blocks, pack_text, 0)
    text_recv[me] = text_send[me]

    @pl.when(section < sections - 1)
    def _():
        pl.semaphore_wait(barrier, seq_count)

    @pl.when(section == sections - 1)
    def _():
        pl.semaphore_wait(barrier, seq_count - 1)

    def send_text(step, carry):
        target = lax.rem(me + step, seq_count)
        push(text_send.at[target], text_recv.at[me], text_send_sem, text_recv_sem, target)
        return carry

    lax.fori_loop(1, seq_count, send_text, 0)

    loads[0].wait()

    def pack_q(step, carry):
        first = lax.rem(my_block + step, blocks) * span
        parts = normed([queries[:, tile(first, at)].astype(F32) for at in pairs], query_gain_both)
        for at, data in zip(pairs, parts):
            data = data.astype(BF16)
            top, bottom = data[0:half], data[half:]
            q_send[first + 2 * at] = jnp.where(below_half, top, swap_halves(bottom))
            q_send[first + 2 * at + 1] = jnp.where(below_half, swap_halves(top), bottom)
        for turn in range(span):
            target = first + lax.rem(my_place + turn, span)
            slot = step * span + turn

            @pl.when(slot > 0)
            def _(target=target, slot=slot):
                push(q_send.at[target], q_recv.at[slot], q_send_sem, q_recv_sem, target)

        return carry

    lax.fori_loop(0, blocks, pack_q, 0)
    q_recv[0] = q_send[me]

    loads[1].wait()
    loads[2].wait()

    def pack_kv(step, carry):
        first = lax.rem(my_block + step, blocks) * span
        parts = normed([keys[:, tile(first, at)].astype(F32) for at in pairs], key_gain_both)
        for at, key in zip(pairs, parts):
            key = key.astype(BF16)
            value = values[:, tile(first, at)]
            kv_send[first + 2 * at] = jnp.where(below, key, swap_halves(value))
            kv_send[first + 2 * at + 1] = jnp.where(below, swap_halves(key), value)
        for turn in range(span):
            target = first + lax.rem(my_place + turn, span)
            slot = step * span + turn

            @pl.when(slot > 0)
            def _(target=target, slot=slot):
                push(kv_send.at[target], kv_recv.at[slot], kv_send_sem, kv_recv_sem.at[step], target)

        return carry

    lax.fori_loop(0, blocks, pack_kv, 0)
    kv_recv[0] = kv_send[me]

    @pl.when(section == 0)
    def _():
        pltpu.make_async_copy(fresh, block_in, shift_recv_sem).start()

    shift = pltpu.make_async_remote_copy(
        stale,
        block_in,
        shift_send_sem,
        shift_recv_sem,
        device_id={"section": lax.rem(section + 1, sections)},
        device_id_type=MESH,
    )

    @pl.when(section < sections - 1)
    def _():
        shift.start()

    def await_slots(recv, count, sem):
        part = recv.at[pl.ds(0, count)]
        pltpu.make_async_copy(part, part, sem).wait()

    def await_step(recv, step, sem):
        @pl.when(step == 0)
        def _():
            await_slots(recv, span - 1, sem.at[0])

        @pl.when(step > 0)
        def _():
            await_slots(recv, span, sem.at[step])

    await_slots(text_recv, seq_count - 1, text_recv_sem)
    live_count = counts[me // (seq_count // 2)]
    text_all = text_recv[...].astype(F32)[:, 0:TEXT_SLOT, :].reshape(text_total, LANES)
    text_k[...] = text_all.astype(BF16)
    place = lax.broadcasted_iota(jnp.int32, (text_total, LANES), 0)
    within = place % TEXT_SLOT
    live = (within < text_rows) & ((place // TEXT_SLOT) * text_rows + within < live_count)
    text_v[...] = jnp.where(
        live, jnp.where(lanes_below_half((text_total, LANES)), 1.0, text_all), 0.0
    ).astype(BF16)
    gate_acc[...] = jnp.zeros_like(gate_acc)

    def collect_gate(step, carry):
        at = (step * gate_span) // LANES
        columns = pl.ds(pl.multiple_of(at * LANES, LANES), LANES)
        gate_acc[:, columns] = gate_acc[:, columns] + text_recv[step].astype(F32)[TEXT_SLOT:]
        return carry

    lax.fori_loop(0, seq_count, collect_gate, 0)

    await_slots(q_recv, seq_count - 1, q_recv_sem)
    left = lanes_below_half((block_rows // 2, LANES))

    def rows_of(block):
        return pl.ds(pl.multiple_of(block * block_rows, block_rows), block_rows)

    def spread(block, carry):
        packed = q_recv[pl.ds(pl.multiple_of(block * span, span), span)].reshape(block_rows // 2, LANES)
        zero = jnp.zeros((), BF16)
        query_rows[rows_of(block), :] = jnp.concatenate(
            [jnp.where(left, packed, zero), jnp.where(left, swap_halves(packed), zero)], axis=0
        )
        return carry

    lax.fori_loop(0, blocks, spread, 0)

    def attend(block, key, value):
        scores = lax.dot_general(
            query_rows[rows_of(block), :], key, (((1,), (1,)), ((), ())), preferred_element_type=F32
        )
        weights = jnp.exp2(scores * SCALE).astype(BF16)
        return jnp.dot(weights, value, preferred_element_type=F32)

    def attend_text(block, carry):
        total[rows_of(block), :] = attend(block, text_k[...], text_v[...])
        return carry

    lax.fori_loop(0, blocks, attend_text, 0)

    def keys_of(step):
        return kv_recv[pl.ds(pl.multiple_of(step * span, span), span)].reshape(block_rows, LANES)

    def prepare(step):
        await_step(kv_recv, step, kv_recv_sem)
        value_aug[...] = jnp.where(lanes_below_half((block_rows, LANES)), jnp.ones((), BF16), keys_of(step))

    def attend_step(step, carry):
        prepare(step)

        def attend_block(block, inner):
            total[rows_of(block), :] += attend(block, keys_of(step), value_aug[...])
            return inner

        lax.fori_loop(0, blocks, attend_block, 0)
        return carry

    lax.fori_loop(0, blocks - 1, attend_step, 0)

    prepare(blocks - 1)

    def finish_block(block, carry):
        summed = total[rows_of(block), :] + attend(block, keys_of(blocks - 1), value_aug[...])
        result = summed / swap_halves(summed)
        top, bottom = result[0 : block_rows // 2], result[block_rows // 2 :]
        mixed = jnp.where(left, swap_halves(top), bottom).astype(BF16)
        o_send[pl.ds(pl.multiple_of(block * span, span), span)] = mixed.reshape(span, half, LANES)
        first = lax.rem(my_block - block + blocks, blocks) * span
        for turn in range(span):
            source = first + lax.rem(my_place - turn + span, span)
            slot = block * span + turn

            @pl.when(slot > 0)
            def _(source=source, slot=slot):
                push(o_send.at[slot], o_recv.at[me], o_send_sem, o_recv_sem.at[block], source)

        return carry

    lax.fori_loop(0, blocks, finish_block, 0)
    o_recv[me] = o_send[0]

    loads[3].wait()
    projected[...] = jnp.zeros_like(projected)

    def project(step, carry):
        await_step(o_recv, step, o_recv_sem)
        block = lax.rem(my_block + step, blocks)
        image = block // (blocks // 2)
        weight_rows = pl.ds(
            pl.multiple_of(lax.rem(block, blocks // 2) * block_columns, block_columns), block_columns
        )
        tops, bottoms = [], []
        for at in pairs:
            one, two = o_recv[block * span + 2 * at], o_recv[block * span + 2 * at + 1]
            tops.append(jnp.where(below_half, one, swap_halves(two)))
            bottoms.append(jnp.where(below_half, swap_halves(one), two))
        attended = jnp.concatenate(
            [jnp.concatenate(tops, axis=1), jnp.concatenate(bottoms, axis=1)], axis=0
        )
        for start in range(0, width, 512):
            stop = min(start + 512, width)
            projected[image, :, start:stop] += jnp.dot(
                attended, weight[weight_rows, start:stop], preferred_element_type=F32
            )
        return carry

    lax.fori_loop(0, blocks, project, 0)

    @pl.when(section == 0)
    def _():
        pltpu.make_async_copy(fresh, block_in, shift_recv_sem).wait()

    @pl.when(section > 0)
    def _():
        shift.wait_recv()

    gate_sum = gate_acc[...]
    gate_next = jnp.concatenate([jnp.zeros((4, LANES), F32), gate_sum[4:8, : width - LANES]], axis=1)
    gate_four = gate_sum[0:4, :width] + gate_next
    gate_vec = gate_four[0:2] + gate_four[2:4]
    for image in range(2):
        held = block_in[image].astype(F32)
        out[image] = (held + gate_vec[image : image + 1] * projected[image]).astype(BF16)

    for send, sem in (
        (text_send, text_send_sem),
        (q_send, q_send_sem),
        (kv_send, kv_send_sem),
        (o_send, o_send_sem),
    ):
        await_slots(send, seq_count - 1, sem)

    @pl.when(section < sections - 1)
    def _():
        shift.wait_send()


def solution(mesh):
    seq_count = mesh.shape["seq"]
    span = 8

    def step(
        stale,
        fresh,
        queries,
        image_keys,
        image_values,
        text_keys,
        text_values,
        text_count,
        timesteps,
        query_gain,
        key_gain,
        out_weight,
        gate_weight,
    ):
        images, rows, width = fresh.shape
        half = rows // 2
        columns = queries.shape[2]
        padded = -(-width // LANES) * LANES + LANES
        blocks = seq_count // span
        vmem = pl.BlockSpec(memory_space=pltpu.VMEM)
        smem = pl.BlockSpec(memory_space=pltpu.SMEM)
        hbm = pl.BlockSpec(memory_space=pl.ANY)
        dma = pltpu.SemaphoreType.DMA
        text_total = seq_count * TEXT_SLOT
        result = pl.pallas_call(
            functools.partial(kernel, seq_count, span),
            out_shape=jax.ShapeDtypeStruct((images, rows, width), BF16),
            in_specs=[smem, smem] + [vmem] * 5 + [hbm] * 6,
            out_specs=vmem,
            scratch_shapes=[
                pltpu.VMEM((rows, columns), BF16),
                pltpu.VMEM((rows, columns), BF16),
                pltpu.VMEM((rows, columns), BF16),
                pltpu.VMEM((seq_count, 2 * TEXT_SLOT, LANES), BF16),
                pltpu.VMEM((seq_count, 2 * TEXT_SLOT, LANES), BF16),
                pltpu.VMEM((seq_count, half, LANES), BF16),
                pltpu.VMEM((seq_count, half, LANES), BF16),
                pltpu.VMEM((seq_count, rows, LANES), BF16),
                pltpu.VMEM((seq_count, rows, LANES), BF16),
                pltpu.VMEM((seq_count, half, LANES), BF16),
                pltpu.VMEM((seq_count, half, LANES), BF16),
                pltpu.VMEM((2, TEXT_SLOT, columns), F32),
                pltpu.VMEM((text_total, LANES), BF16),
                pltpu.VMEM((text_total, LANES), BF16),
                pltpu.VMEM((span * rows, LANES), BF16),
                pltpu.VMEM((seq_count * rows, LANES), BF16),
                pltpu.VMEM((seq_count * rows, LANES), F32),
                pltpu.VMEM((8, 2 * LANES), F32),
                pltpu.VMEM((8, padded), F32),
                pltpu.VMEM(out_weight.shape[1:], BF16),
                pltpu.VMEM((images, rows, width), BF16),
                pltpu.VMEM((images, rows, width), F32),
                dma((4,)),
                dma,
                dma,
                dma,
                dma,
                dma,
                dma((blocks,)),
                dma,
                dma((blocks,)),
                dma,
                dma,
            ],
            compiler_params=pltpu.CompilerParams(
                collective_id=0, has_side_effects=True, vmem_limit_bytes=56 * 1024 * 1024
            ),
            name="joint_attention",
        )(
            text_count,
            timesteps[0],
            text_keys[0],
            text_values[0],
            query_gain,
            key_gain,
            gate_weight[0].T,
            queries[0],
            image_keys[0],
            image_values[0],
            out_weight[0],
            stale[0],
            fresh,
        )
        return result[None]

    return jax.shard_map(
        step,
        mesh=mesh,
        in_specs=(
            P("section", None, "seq", None),
            P(None, "seq", None),
            P("section", "seq", None),
            P("section", "seq", None),
            P("section", "seq", None),
            P("section", "seq", None),
            P("section", "seq", None),
            P(),
            P("section", None),
            P("section", None),
            P("section", None),
            P("section", None, None),
            P("section", None, "seq"),
        ),
        out_specs=P("section", None, "seq", None),
        check_vma=False,
    )
```

time: 102 us -> 87.9 us (0.86); the launches traced: 102 us -> 86.8 us
  Pallas kernels: 96.1 us -> 84.9 us
  local copies, waits for them, and re-layouts: 5.97 us -> 1.95 us
    pallas_call x1, Pallas kernels: 96.1 us -> 84.9 us  [step(): pl.pallas_call(functools.partial(kernel, seq_count, span), out_shape=jax....]
    another operation x4 -> x0, local copies, waits for them, and re-layouts: 2.55 us -> none  [the longest x2 1.31 us: step(): jnp.tile(query_gain, (1, 2))]
    unnamed x2 -> x1, local copies, waits for them, and re-layouts: 3.42 us -> 1.95 us
where the time goes in v2:
time: 87.9 us; the launch traced here: 86.8 us
  Pallas kernels  84.9 us (97%)
  local copies, waits for them, and re-layouts  1.95 us (2%)
    pallas_call x1, Pallas kernels, step(): pl.pallas_call(functools.partial(kernel, seq_count, span), out_shape=jax....  84.9 us
    unnamed x1, local copies, waits for them, and re-layouts  1.95 us

profile of v2, /device:TPU:1, one launch (start us, length us, event | category | flops | bytes accessed | tf_op | source)
XLA Modules:
  0.0 86.8 jit_solution(10717542029933170032)
XLA Ops:
  0.0 84.9 %joint_attention.1 = bf16[2,64,2432]{2,1,0:T(8,128)(2,1)} custom-call(s32[2]{0:T(128)} %counts.1, s32[2]{0:T(128)} %bitcast.21, bf16[6,4096]{1,0:T(8,128)(2,1)} %bitcast.18, bf16[6,4096]{1,0:T(8,128)(2,1)} %bitcast.19, f32[1,64]{1,0:T(1,128)} %query_gain.1, f32[1,64]{1,0:T(1,128)} %key_gain.1, bf16[38,256]{1,0:T(8,128)(2,1)} %bitcast.20, ...), custom_call_target="tpu_custom_call" | custom-call | tf_op jit(solution)/shard_map/joint_attention/pallas_call | solution.py:452
  84.9 1.9 %copy.15 = bf16[1,2,64,2432]{3,2,1,0:T(8,128)(2,1)} copy(bf16[1,2,64,2432]{3,2,1,0:T(8,128)(2,1)} %bitcast.13) | data formatting | bytes 1245184

commit v3 on v2

--- a/solution.py
+++ b/solution.py
@@ -43,6 +43,7 @@
 def kernel(
     seq_count,
     span,
+    early,
     counts,
     times,
     text_keys,
@@ -98,10 +99,18 @@
     half = rows // 2
     text_rows = text_keys.shape[0]
     blocks = seq_count // span
-    my_block, my_place = me // span, lax.rem(me, span)
+    my_block = (me // 16) * 2 + (me % 4) // 2
+    my_place = ((me // 4) % 4) * 2 + me % 2
+    my_label = my_block * span + my_place
+
+    def device_at(block, place):
+        return (block // 2) * 16 + (place // 2) * 4 + (block % 2) * 2 + place % 2
+
+    def tile_index(block, at):
+        return (block // 2) * 8 + at * 2 + block % 2
+
     pairs = range(span // 2)
     block_rows = span * rows
-    block_columns = span * HD
     gate_span = gate_weight.shape[0]
     width = out.shape[2]
     text_total = seq_count * TEXT_SLOT
@@ -145,23 +154,16 @@
     gate_pad[:, 0:gate_span] = lax.dot_general(
         activated, gate_weight[...], (((1,), (1,)), ((), ())), preferred_element_type=F32
     )
-    gate_row = pltpu.roll(gate_pad[...], lax.rem(me * gate_span, LANES), 1)
-    gate_high = gate_row.astype(BF16).astype(F32)
-    gate_low = gate_row - gate_high
-    gate_rows = jnp.where(
-        row8 < 2,
-        gate_high[:, :LANES],
-        jnp.where(
-            row8 < 4, gate_low[:, :LANES], jnp.where(row8 < 6, gate_high[:, LANES:], gate_low[:, LANES:])
-        ),
-    )
+    gate_share = gate_pad[...]
+    gate_high = gate_share.astype(BF16).astype(F32)
+    gate_rows = jnp.where(lane8 < HD, gate_high, swap_halves(gate_share - gate_high))
 
     below = lanes_below_half((rows, LANES))
     below8 = lanes_below_half((TEXT_SLOT, LANES))
     below_half = lanes_below_half((half, LANES))
 
-    def tile(first, at):
-        return pl.ds(pl.multiple_of(first * HD + at * LANES, LANES), LANES)
+    def tile(index):
+        return pl.ds(pl.multiple_of(index * LANES, LANES), LANES)
 
     def push(send, recv, send_sem, recv_sem, target):
         pltpu.make_async_remote_copy(
@@ -170,13 +172,13 @@
 
     def pack_text(step, carry):
         first = step * span
-        normed_keys = normed([text_pad[0, :, tile(first, at)] for at in pairs], key_gain_both)
+        normed_keys = normed([text_pad[0, :, tile(first // 2 + at)] for at in pairs], key_gain_both)
         for at, text_key in zip(pairs, normed_keys):
-            text_value = text_pad[1, :, tile(first, at)]
+            text_value = text_pad[1, :, tile(first // 2 + at)]
             one = jnp.where(below8, text_key, swap_halves(text_value))
             two = jnp.where(below8, swap_halves(text_key), text_value)
-            text_send[first + 2 * at] = jnp.concatenate([one, gate_rows], axis=0).astype(BF16)
-            text_send[first + 2 * at + 1] = jnp.concatenate([two, gate_rows], axis=0).astype(BF16)
+            text_send[first + 2 * at] = jnp.where(row8 < text_rows, one, gate_rows).astype(BF16)
+            text_send[first + 2 * at + 1] = jnp.where(row8 < text_rows, two, gate_rows).astype(BF16)
         return carry
 
     lax.fori_loop(0, blocks, pack_text, 0)
@@ -200,49 +202,65 @@
     loads[0].wait()
 
     def pack_q(step, carry):
-        first = lax.rem(my_block + step, blocks) * span
-        parts = normed([queries[:, tile(first, at)].astype(F32) for at in pairs], query_gain_both)
+        block = lax.rem(my_block + step, blocks)
+        first = block * span
+        parts = normed([queries[:, tile(tile_index(block, at))].astype(F32) for at in pairs], query_gain_both)
         for at, data in zip(pairs, parts):
             data = data.astype(BF16)
             top, bottom = data[0:half], data[half:]
             q_send[first + 2 * at] = jnp.where(below_half, top, swap_halves(bottom))
             q_send[first + 2 * at + 1] = jnp.where(below_half, swap_halves(top), bottom)
         for turn in range(span):
-            target = first + lax.rem(my_place + turn, span)
+            place = lax.rem(my_place + turn, span)
             slot = step * span + turn
 
             @pl.when(slot > 0)
-            def _(target=target, slot=slot):
-                push(q_send.at[target], q_recv.at[slot], q_send_sem, q_recv_sem, target)
-
-        return carry
-
-    lax.fori_loop(0, blocks, pack_q, 0)
-    q_recv[0] = q_send[me]
+            def _(place=place, slot=slot):
+                push(
+                    q_send.at[first + place],
+                    q_recv.at[slot],
+                    q_send_sem,
+                    q_recv_sem.at[step],
+                    device_at(block, place),
+                )
+
+        return carry
+
+    lax.fori_loop(0, early, pack_q, 0)
+    q_recv[0] = q_send[my_label]
 
     loads[1].wait()
     loads[2].wait()
 
     def pack_kv(step, carry):
-        first = lax.rem(my_block + step, blocks) * span
-        parts = normed([keys[:, tile(first, at)].astype(F32) for at in pairs], key_gain_both)
+        block = lax.rem(my_block + step, blocks)
+        first = block * span
+        parts = normed([keys[:, tile(tile_index(block, at))].astype(F32) for at in pairs], key_gain_both)
         for at, key in zip(pairs, parts):
             key = key.astype(BF16)
-            value = values[:, tile(first, at)]
+            value = values[:, tile(tile_index(block, at))]
             kv_send[first + 2 * at] = jnp.where(below, key, swap_halves(value))
             kv_send[first + 2 * at + 1] = jnp.where(below, swap_halves(key), value)
         for turn in range(span):
-            target = first + lax.rem(my_place + turn, span)
+            place = lax.rem(my_place + turn, span)
             slot = step * span + turn
 
             @pl.when(slot > 0)
-            def _(target=target, slot=slot):
-                push(kv_send.at[target], kv_recv.at[slot], kv_send_sem, kv_recv_sem.at[step], target)
+            def _(place=place, slot=slot):
+                push(
+                    kv_send.at[first + place],
+                    kv_recv.at[slot],
+                    kv_send_sem,
+                    kv_recv_sem.at[step],
+                    device_at(block, place),
+                )
 
         return carry
 
     lax.fori_loop(0, blocks, pack_kv, 0)
-    kv_recv[0] = kv_send[me]
+    kv_recv[0] = kv_send[my_label]
+
+    lax.fori_loop(early, blocks, pack_q, 0)
 
     @pl.when(section == 0)
     def _():
@@ -266,6 +284,10 @@
         pltpu.make_async_copy(part, part, sem).wait()
 
     def await_step(recv, step, sem):
+        if isinstance(step, int):
+            await_slots(recv, span if step else span - 1, sem.at[step])
+            return
+
         @pl.when(step == 0)
         def _():
             await_slots(recv, span - 1, sem.at[0])
@@ -276,39 +298,45 @@
 
     await_slots(text_recv, seq_count - 1, text_recv_sem)
     live_count = counts[me // (seq_count // 2)]
-    text_all = text_recv[...].astype(F32)[:, 0:TEXT_SLOT, :].reshape(text_total, LANES)
-    text_k[...] = text_all.astype(BF16)
+    text_all = text_recv[...].astype(F32).reshape(text_total, LANES)
     place = lax.broadcasted_iota(jnp.int32, (text_total, LANES), 0)
     within = place % TEXT_SLOT
+    text_k[...] = jnp.where(within < text_rows, text_all, 0.0).astype(BF16)
     live = (within < text_rows) & ((place // TEXT_SLOT) * text_rows + within < live_count)
     text_v[...] = jnp.where(
         live, jnp.where(lanes_below_half((text_total, LANES)), 1.0, text_all), 0.0
     ).astype(BF16)
-    gate_acc[...] = jnp.zeros_like(gate_acc)
-
-    def collect_gate(step, carry):
-        at = (step * gate_span) // LANES
-        columns = pl.ds(pl.multiple_of(at * LANES, LANES), LANES)
-        gate_acc[:, columns] = gate_acc[:, columns] + text_recv[step].astype(F32)[TEXT_SLOT:]
-        return carry
-
-    lax.fori_loop(0, seq_count, collect_gate, 0)
-
-    await_slots(q_recv, seq_count - 1, q_recv_sem)
+    gate_tiles = [jnp.zeros((TEXT_SLOT, LANES), F32) for _ in range(width // LANES)]
+    for source in range(seq_count):
+        at, ahead = divmod(source * gate_span, LANES)
+        share = text_recv[source].astype(F32)
+        share = jnp.where(below8, share + swap_halves(share), 0.0)
+        if ahead > 0:
+            share = pltpu.roll(share, ahead, 1)
+        if ahead + gate_span > LANES:
+            gate_tiles[at + 1] = gate_tiles[at + 1] + jnp.where(lane8 < ahead, share, 0.0)
+            share = jnp.where(lane8 < ahead, 0.0, share)
+        gate_tiles[at] = gate_tiles[at] + share
+    for at, gate_tile in enumerate(gate_tiles):
+        gate_acc[:, at * LANES : (at + 1) * LANES] = gate_tile
+
     left = lanes_below_half((block_rows // 2, LANES))
 
     def rows_of(block):
-        return pl.ds(pl.multiple_of(block * block_rows, block_rows), block_rows)
-
-    def spread(block, carry):
-        packed = q_recv[pl.ds(pl.multiple_of(block * span, span), span)].reshape(block_rows // 2, LANES)
+        start = block * block_rows
+        return pl.ds(start if isinstance(start, int) else pl.multiple_of(start, block_rows), block_rows)
+
+    def slots_of(block):
+        start = block * span
+        return pl.ds(start if isinstance(start, int) else pl.multiple_of(start, span), span)
+
+    def spread(block):
+        await_step(q_recv, block, q_recv_sem)
+        packed = q_recv[slots_of(block)].reshape(block_rows // 2, LANES)
         zero = jnp.zeros((), BF16)
         query_rows[rows_of(block), :] = jnp.concatenate(
             [jnp.where(left, packed, zero), jnp.where(left, swap_halves(packed), zero)], axis=0
         )
-        return carry
-
-    lax.fori_loop(0, blocks, spread, 0)
 
     def attend(block, key, value):
         scores = lax.dot_general(
@@ -317,52 +345,56 @@
         weights = jnp.exp2(scores * SCALE).astype(BF16)
         return jnp.dot(weights, value, preferred_element_type=F32)
 
-    def attend_text(block, carry):
-        total[rows_of(block), :] = attend(block, text_k[...], text_v[...])
-        return carry
-
-    lax.fori_loop(0, blocks, attend_text, 0)
-
     def keys_of(step):
-        return kv_recv[pl.ds(pl.multiple_of(step * span, span), span)].reshape(block_rows, LANES)
+        return kv_recv[slots_of(step)].reshape(block_rows, LANES)
 
     def prepare(step):
         await_step(kv_recv, step, kv_recv_sem)
-        value_aug[...] = jnp.where(lanes_below_half((block_rows, LANES)), jnp.ones((), BF16), keys_of(step))
-
-    def attend_step(step, carry):
-        prepare(step)
-
-        def attend_block(block, inner):
-            total[rows_of(block), :] += attend(block, keys_of(step), value_aug[...])
-            return inner
-
-        lax.fori_loop(0, blocks, attend_block, 0)
-        return carry
-
-    lax.fori_loop(0, blocks - 1, attend_step, 0)
-
-    prepare(blocks - 1)
-
-    def finish_block(block, carry):
-        summed = total[rows_of(block), :] + attend(block, keys_of(blocks - 1), value_aug[...])
+        value_aug[rows_of(step), :] = jnp.where(
+            lanes_below_half((block_rows, LANES)), jnp.ones((), BF16), keys_of(step)
+        )
+
+    def attend_step(block, step):
+        return attend(block, keys_of(step), value_aug[rows_of(step), :])
+
+    def finish(block, summed):
         result = summed / swap_halves(summed)
         top, bottom = result[0 : block_rows // 2], result[block_rows // 2 :]
         mixed = jnp.where(left, swap_halves(top), bottom).astype(BF16)
-        o_send[pl.ds(pl.multiple_of(block * span, span), span)] = mixed.reshape(span, half, LANES)
-        first = lax.rem(my_block - block + blocks, blocks) * span
+        o_send[slots_of(block)] = mixed.reshape(span, half, LANES)
+        from_block = lax.rem(my_block - block + blocks, blocks)
         for turn in range(span):
-            source = first + lax.rem(my_place - turn + span, span)
+            source = device_at(from_block, lax.rem(my_place - turn + span, span))
             slot = block * span + turn
-
-            @pl.when(slot > 0)
-            def _(source=source, slot=slot):
-                push(o_send.at[slot], o_recv.at[me], o_send_sem, o_recv_sem.at[block], source)
-
-        return carry
-
-    lax.fori_loop(0, blocks, finish_block, 0)
-    o_recv[me] = o_send[0]
+            if not isinstance(slot, int) or slot > 0:
+                push(o_send.at[slot], o_recv.at[my_label], o_send_sem, o_recv_sem.at[block], source)
+
+    for block in range(early):
+        spread(block)
+    for block in range(early):
+        total[rows_of(block), :] = attend(block, text_k[...], text_v[...])
+
+    def meet(step, carry):
+        prepare(step)
+        for block in range(early):
+            total[rows_of(block), :] += attend_step(block, step)
+        return carry
+
+    lax.fori_loop(0, blocks - 1, meet, 0)
+    prepare(blocks - 1)
+    for block in range(early):
+        finish(block, total[rows_of(block), :] + attend_step(block, blocks - 1))
+
+    def attend_all(block, carry):
+        spread(block)
+        summed = attend(block, text_k[...], text_v[...])
+        for step in range(blocks):
+            summed = summed + attend_step(block, step)
+        finish(block, summed)
+        return carry
+
+    lax.fori_loop(early, blocks, attend_all, 0)
+    o_recv[my_label] = o_send[0]
 
     loads[3].wait()
     projected[...] = jnp.zeros_like(projected)
@@ -371,9 +403,7 @@
         await_step(o_recv, step, o_recv_sem)
         block = lax.rem(my_block + step, blocks)
         image = block // (blocks // 2)
-        weight_rows = pl.ds(
-            pl.multiple_of(lax.rem(block, blocks // 2) * block_columns, block_columns), block_columns
-        )
+        weight_tiles = [tile(lax.rem(tile_index(block, at), seq_count // 4)) for at in pairs]
         tops, bottoms = [], []
         for at in pairs:
             one, two = o_recv[block * span + 2 * at], o_recv[block * span + 2 * at + 1]
@@ -384,9 +414,8 @@
         )
         for start in range(0, width, 512):
             stop = min(start + 512, width)
-            projected[image, :, start:stop] += jnp.dot(
-                attended, weight[weight_rows, start:stop], preferred_element_type=F32
-            )
+            part = jnp.concatenate([weight[part_rows, start:stop] for part_rows in weight_tiles], axis=0)
+            projected[image, :, start:stop] += jnp.dot(attended, part, preferred_element_type=F32)
         return carry
 
     lax.fori_loop(0, blocks, project, 0)
@@ -399,10 +428,7 @@
     def _():
         shift.wait_recv()
 
-    gate_sum = gate_acc[...]
-    gate_next = jnp.concatenate([jnp.zeros((4, LANES), F32), gate_sum[4:8, : width - LANES]], axis=1)
-    gate_four = gate_sum[0:4, :width] + gate_next
-    gate_vec = gate_four[0:2] + gate_four[2:4]
+    gate_vec = gate_acc[text_rows : text_rows + 2, :]
     for image in range(2):
         held = block_in[image].astype(F32)
         out[image] = (held + gate_vec[image : image + 1] * projected[image]).astype(BF16)
@@ -423,6 +449,7 @@
 def solution(mesh):
     seq_count = mesh.shape["seq"]
     span = 8
+    early = 6
 
     def step(
         stale,
@@ -442,7 +469,6 @@
         images, rows, width = fresh.shape
         half = rows // 2
         columns = queries.shape[2]
-        padded = -(-width // LANES) * LANES + LANES
         blocks = seq_count // span
         vmem = pl.BlockSpec(memory_space=pltpu.VMEM)
         smem = pl.BlockSpec(memory_space=pltpu.SMEM)
@@ -450,16 +476,16 @@
         dma = pltpu.SemaphoreType.DMA
         text_total = seq_count * TEXT_SLOT
         result = pl.pallas_call(
-            functools.partial(kernel, seq_count, span),
-            out_shape=jax.ShapeDtypeStruct((images, rows, width), BF16),
+            functools.partial(kernel, seq_count, span, early),
+            out_shape=pltpu.VMEM((images, rows, width), BF16),
             in_specs=[smem, smem] + [vmem] * 5 + [hbm] * 6,
             out_specs=vmem,
             scratch_shapes=[
                 pltpu.VMEM((rows, columns), BF16),
                 pltpu.VMEM((rows, columns), BF16),
                 pltpu.VMEM((rows, columns), BF16),
-                pltpu.VMEM((seq_count, 2 * TEXT_SLOT, LANES), BF16),
-                pltpu.VMEM((seq_count, 2 * TEXT_SLOT, LANES), BF16),
+                pltpu.VMEM((seq_count, TEXT_SLOT, LANES), BF16),
+                pltpu.VMEM((seq_count, TEXT_SLOT, LANES), BF16),
                 pltpu.VMEM((seq_count, half, LANES), BF16),
                 pltpu.VMEM((seq_count, half, LANES), BF16),
                 pltpu.VMEM((seq_count, rows, LANES), BF16),
@@ -469,11 +495,11 @@
                 pltpu.VMEM((2, TEXT_SLOT, columns), F32),
                 pltpu.VMEM((text_total, LANES), BF16),
                 pltpu.VMEM((text_total, LANES), BF16),
-                pltpu.VMEM((span * rows, LANES), BF16),
                 pltpu.VMEM((seq_count * rows, LANES), BF16),
-                pltpu.VMEM((seq_count * rows, LANES), F32),
-                pltpu.VMEM((8, 2 * LANES), F32),
-                pltpu.VMEM((8, padded), F32),
+                pltpu.VMEM((seq_count * rows, LANES), BF16),
+                pltpu.VMEM((early * span * rows, LANES), F32),
+                pltpu.VMEM((TEXT_SLOT, LANES), F32),
+                pltpu.VMEM((TEXT_SLOT, width), F32),
                 pltpu.VMEM(out_weight.shape[1:], BF16),
                 pltpu.VMEM((images, rows, width), BF16),
                 pltpu.VMEM((images, rows, width), F32),
@@ -481,7 +507,7 @@
                 dma,
                 dma,
                 dma,
-                dma,
+                dma((blocks,)),
                 dma,
                 dma((blocks,)),
                 dma,

time: 87.9 us -> 74.2 us (0.84); the launches traced: 86.8 us -> 74.1 us
  Pallas kernels: 84.9 us -> 73.2 us
  local copies, waits for them, and re-layouts: 1.95 us -> 0.83 us
    pallas_call x1, Pallas kernels: 84.9 us -> 73.2 us  [step(): pl.pallas_call(functools.partial(kernel, seq_count, span, early), out_sha...]
    unnamed x1, local copies, waits for them, and re-layouts: 1.95 us -> 0.83 us
where the time goes in v3:
time: 74.2 us; the launch traced here: 74.1 us
  Pallas kernels  73.2 us (99%)
  local copies, waits for them, and re-layouts  0.83 us (1%)
    pallas_call x1, Pallas kernels, step(): pl.pallas_call(functools.partial(kernel, seq_count, span, early), out_sha...  73.2 us

profile of v3, /device:TPU:1, one launch (start us, length us, event | category | flops | bytes accessed | tf_op | source)
XLA Modules:
  0.0 74.1 jit_solution(11158156974107589769)
XLA Ops:
  0.0 73.2 %joint_attention.1 = bf16[2,64,2432]{2,1,0:T(8,128)(2,1)S(1)} custom-call(s32[2]{0:T(128)} %counts.1, s32[2]{0:T(128)} %bitcast.21, bf16[6,4096]{1,0:T(8,128)(2,1)} %bitcast.18, bf16[6,4096]{1,0:T(8,128)(2,1)} %bitcast.19, f32[1,64]{1,0:T(1,128)} %query_gain.1, f32[1,64]{1,0:T(1,128)} %key_gain.1, bf16[38,256]{1,0:T(8,128)(2,1)} %bitcast.20, ...), custom_call_target="tpu_custom_call" | custom-call | tf_op jit(solution)/shard_map/joint_attention/pallas_call | solution.py:478
  73.3 0.8 %copy.15 = bf16[1,2,64,2432]{3,2,1,0:T(8,128)(2,1)} copy(bf16[1,2,64,2432]{3,2,1,0:T(8,128)(2,1)S(1)} %bitcast.12) | data formatting | bytes 1245184

commit v4 on v3

--- a/solution.py
+++ b/solution.py
@@ -46,11 +46,11 @@
     early,
     counts,
     times,
-    text_keys,
-    text_values,
-    query_gain,
-    key_gain,
-    gate_weight,
+    text_keys_hbm,
+    text_values_hbm,
+    query_gain_hbm,
+    key_gain_hbm,
+    gate_weight_hbm,
     queries_hbm,
     keys_hbm,
     values_hbm,
@@ -58,6 +58,11 @@
     stale,
     fresh,
     out,
+    text_keys,
+    text_values,
+    query_gain,
+    key_gain,
+    gate_weight,
     queries,
     keys,
     values,
@@ -102,6 +107,7 @@
     my_block = (me // 16) * 2 + (me % 4) // 2
     my_place = ((me // 4) % 4) * 2 + me % 2
     my_label = my_block * span + my_place
+    way = 1 - 2 * (section % 2)
 
     def device_at(block, place):
         return (block // 2) * 16 + (place // 2) * 4 + (block % 2) * 2 + place % 2
@@ -110,6 +116,7 @@
         return (block // 2) * 8 + at * 2 + block % 2
 
     pairs = range(span // 2)
+    turns = [2, 6, 4, 0, 3, 7, 5, 1]
     block_rows = span * rows
     gate_span = gate_weight.shape[0]
     width = out.shape[2]
@@ -130,13 +137,25 @@
         pl.semaphore_signal(barrier, inc=1, device_id={"section": section - 1}, device_id_type=MESH)
 
     loads = [
-        pltpu.make_async_copy(queries_hbm, queries, load_sem.at[0]),
-        pltpu.make_async_copy(keys_hbm, keys, load_sem.at[1]),
-        pltpu.make_async_copy(values_hbm, values, load_sem.at[2]),
-        pltpu.make_async_copy(out_weight, weight, load_sem.at[3]),
+        pltpu.make_async_copy(source, target, load_sem.at[at])
+        for at, (source, target) in enumerate(
+            (
+                (queries_hbm, queries),
+                (keys_hbm, keys),
+                (values_hbm, values),
+                (out_weight, weight),
+                (text_keys_hbm, text_keys),
+                (text_values_hbm, text_values),
+                (query_gain_hbm, query_gain),
+                (key_gain_hbm, key_gain),
+                (gate_weight_hbm, gate_weight),
+            )
+        )
     ]
-    for load in loads:
+    for load in loads[4:] + loads[:4]:
         load.start()
+    for load in loads[4:]:
+        load.wait()
 
     text_pad[...] = jnp.zeros_like(text_pad)
     text_pad[0, 0:text_rows, :] = text_keys[...].astype(F32)
@@ -202,7 +221,7 @@
     loads[0].wait()
 
     def pack_q(step, carry):
-        block = lax.rem(my_block + step, blocks)
+        block = lax.rem(my_block + step * way + blocks, blocks)
         first = block * span
         parts = normed([queries[:, tile(tile_index(block, at))].astype(F32) for at in pairs], query_gain_both)
         for at, data in zip(pairs, parts):
@@ -210,8 +229,8 @@
             top, bottom = data[0:half], data[half:]
             q_send[first + 2 * at] = jnp.where(below_half, top, swap_halves(bottom))
             q_send[first + 2 * at + 1] = jnp.where(below_half, swap_halves(top), bottom)
-        for turn in range(span):
-            place = lax.rem(my_place + turn, span)
+        for turn in turns:
+            place = lax.rem(my_place + turn * way + span, span)
             slot = step * span + turn
 
             @pl.when(slot > 0)
@@ -233,7 +252,7 @@
     loads[2].wait()
 
     def pack_kv(step, carry):
-        block = lax.rem(my_block + step, blocks)
+        block = lax.rem(my_block + step * way + blocks, blocks)
         first = block * span
         parts = normed([keys[:, tile(tile_index(block, at))].astype(F32) for at in pairs], key_gain_both)
         for at, key in zip(pairs, parts):
@@ -241,8 +260,8 @@
             value = values[:, tile(tile_index(block, at))]
             kv_send[first + 2 * at] = jnp.where(below, key, swap_halves(value))
             kv_send[first + 2 * at + 1] = jnp.where(below, swap_halves(key), value)
-        for turn in range(span):
-            place = lax.rem(my_place + turn, span)
+        for turn in turns:
+            place = lax.rem(my_place + turn * way + span, span)
             slot = step * span + turn
 
             @pl.when(slot > 0)
@@ -362,9 +381,9 @@
         top, bottom = result[0 : block_rows // 2], result[block_rows // 2 :]
         mixed = jnp.where(left, swap_halves(top), bottom).astype(BF16)
         o_send[slots_of(block)] = mixed.reshape(span, half, LANES)
-        from_block = lax.rem(my_block - block + blocks, blocks)
-        for turn in range(span):
-            source = device_at(from_block, lax.rem(my_place - turn + span, span))
+        from_block = lax.rem(my_block - block * way + blocks, blocks)
+        for turn in turns:
+            source = device_at(from_block, lax.rem(my_place - turn * way + span, span))
             slot = block * span + turn
             if not isinstance(slot, int) or slot > 0:
                 push(o_send.at[slot], o_recv.at[my_label], o_send_sem, o_recv_sem.at[block], source)
@@ -398,27 +417,36 @@
 
     loads[3].wait()
     projected[...] = jnp.zeros_like(projected)
-
-    def project(step, carry):
+    spans = [(start, min(start + 512, width)) for start in range(0, width, 512)]
+
+    def heads_of(step):
+        block = lax.rem(my_block + step * way + blocks, blocks)
+        return block, block // (blocks // 2)
+
+    def arrived(step, block):
         await_step(o_recv, step, o_recv_sem)
-        block = lax.rem(my_block + step, blocks)
-        image = block // (blocks // 2)
-        weight_tiles = [tile(lax.rem(tile_index(block, at), seq_count // 4)) for at in pairs]
         tops, bottoms = [], []
         for at in pairs:
             one, two = o_recv[block * span + 2 * at], o_recv[block * span + 2 * at + 1]
             tops.append(jnp.where(below_half, one, swap_halves(two)))
             bottoms.append(jnp.where(below_half, swap_halves(one), two))
-        attended = jnp.concatenate(
+        return jnp.concatenate(
             [jnp.concatenate(tops, axis=1), jnp.concatenate(bottoms, axis=1)], axis=0
         )
-        for start in range(0, width, 512):
-            stop = min(start + 512, width)
-            part = jnp.concatenate([weight[part_rows, start:stop] for part_rows in weight_tiles], axis=0)
-            projected[image, :, start:stop] += jnp.dot(attended, part, preferred_element_type=F32)
-        return carry
-
-    lax.fori_loop(0, blocks, project, 0)
+
+    def product(attended, block, start, stop):
+        weight_tiles = [tile(lax.rem(tile_index(block, at), seq_count // 4)) for at in pairs]
+        part = jnp.concatenate([weight[part_rows, start:stop] for part_rows in weight_tiles], axis=0)
+        return jnp.dot(attended, part, preferred_element_type=F32)
+
+    def project(step, carry):
+        block, image = heads_of(step)
+        attended = arrived(step, block)
+        for start, stop in spans:
+            projected[image, :, start:stop] += product(attended, block, start, stop)
+        return carry
+
+    lax.fori_loop(0, blocks - 1, project, 0)
 
     @pl.when(section == 0)
     def _():
@@ -428,10 +456,17 @@
     def _():
         shift.wait_recv()
 
-    gate_vec = gate_acc[text_rows : text_rows + 2, :]
-    for image in range(2):
-        held = block_in[image].astype(F32)
-        out[image] = (held + gate_vec[image : image + 1] * projected[image]).astype(BF16)
+    def mix(image, start, stop, summed):
+        gate = gate_acc[pl.ds(text_rows + image, 1), start:stop]
+        held = block_in[image, :, start:stop].astype(F32)
+        out[image, :, start:stop] = (held + gate * summed).astype(BF16)
+
+    block, image = heads_of(blocks - 1)
+    for start, stop in spans:
+        mix(1 - image, start, stop, projected[1 - image, :, start:stop])
+    attended = arrived(blocks - 1, block)
+    for start, stop in spans:
+        mix(image, start, stop, projected[image, :, start:stop] + product(attended, block, start, stop))
 
     for send, sem in (
         (text_send, text_send_sem),
@@ -478,9 +513,14 @@
         result = pl.pallas_call(
             functools.partial(kernel, seq_count, span, early),
             out_shape=pltpu.VMEM((images, rows, width), BF16),
-            in_specs=[smem, smem] + [vmem] * 5 + [hbm] * 6,
+            in_specs=[smem, smem] + [hbm] * 11,
             out_specs=vmem,
             scratch_shapes=[
+                pltpu.VMEM(text_keys.shape[1:], BF16),
+                pltpu.VMEM(text_values.shape[1:], BF16),
+                pltpu.VMEM(query_gain.shape, F32),
+                pltpu.VMEM(key_gain.shape, F32),
+                pltpu.VMEM(gate_weight.shape[:0:-1], BF16),
                 pltpu.VMEM((rows, columns), BF16),
                 pltpu.VMEM((rows, columns), BF16),
                 pltpu.VMEM((rows, columns), BF16),
@@ -503,7 +543,7 @@
                 pltpu.VMEM(out_weight.shape[1:], BF16),
                 pltpu.VMEM((images, rows, width), BF16),
                 pltpu.VMEM((images, rows, width), F32),
-                dma((4,)),
+                dma((9,)),
                 dma,
                 dma,
                 dma,

time: 74.2 us -> 73.3 us (0.988); the launches traced: 74.1 us -> 72 us
  Pallas kernels: 73.2 us -> 71.2 us
    pallas_call x1, Pallas kernels: 73.2 us -> 71.2 us  [step(): pl.pallas_call(functools.partial(kernel, seq_count, span, early), out_sha...]
where the time goes in v4:
time: 73.3 us; the launch traced here: 72 us
  Pallas kernels  71.2 us (97%)
  local copies, waits for them, and re-layouts  0.83 us (1%)
    pallas_call x1, Pallas kernels, step(): pl.pallas_call(functools.partial(kernel, seq_count, span, early), out_sha...  71.2 us

profile of v4, /device:TPU:1, one launch (start us, length us, event | category | flops | bytes accessed | tf_op | source)
XLA Modules:
  0.0 72.0 jit_solution(9927554548018037425)
XLA Ops:
  0.0 71.2 %joint_attention.1 = bf16[2,64,2432]{2,1,0:T(8,128)(2,1)S(1)} custom-call(s32[2]{0:T(128)} %counts.1, s32[2]{0:T(128)} %bitcast.21, bf16[6,4096]{1,0:T(8,128)(2,1)} %bitcast.18, bf16[6,4096]{1,0:T(8,128)(2,1)} %bitcast.19, f32[1,64]{1,0:T(1,128)} %query_gain_hbm.1, f32[1,64]{1,0:T(1,128)} %key_gain_hbm.1, bf16[38,256]{1,0:T(8,128)(2,1)} %bitcast.20, ...), custom_call_target="tpu_custom_call" | custom-call | tf_op jit(solution)/shard_map/joint_attention/pallas_call | solution.py:513
  71.2 0.8 %copy.15 = bf16[1,2,64,2432]{3,2,1,0:T(8,128)(2,1)} copy(bf16[1,2,64,2432]{3,2,1,0:T(8,128)(2,1)S(1)} %bitcast.12) | data formatting | bytes 1245184

commit v5 on v4

--- a/solution.py
+++ b/solution.py
@@ -189,6 +189,51 @@
             send, recv, send_sem, recv_sem, device_id={"seq": target}, device_id_type=MESH
         ).start()
 
+    loads[0].wait()
+
+    def pack_q(step, carry):
+        block = lax.rem(my_block + step * way + blocks, blocks)
+        first = block * span
+        parts = normed([queries[:, tile(tile_index(block, at))].astype(F32) for at in pairs], query_gain_both)
+        for at, data in zip(pairs, parts):
+            data = data.astype(BF16)
+            top, bottom = data[0:half], data[half:]
+            q_send[first + 2 * at] = jnp.where(below_half, top, swap_halves(bottom))
+            q_send[first + 2 * at + 1] = jnp.where(below_half, swap_halves(top), bottom)
+        return carry
+
+    lax.fori_loop(0, blocks, pack_q, 0)
+    q_recv[0] = q_send[my_label]
+
+    @pl.when(section < sections - 1)
+    def _():
+        pl.semaphore_wait(barrier, seq_count)
+
+    @pl.when(section == sections - 1)
+    def _():
+        pl.semaphore_wait(barrier, seq_count - 1)
+
+    def send_q(step, carry):
+        block = lax.rem(my_block + step * way + blocks, blocks)
+        first = block * span
+        for turn in turns:
+            place = lax.rem(my_place + turn * way + span, span)
+            slot = step * span + turn
+
+            @pl.when(slot > 0)
+            def _(place=place, slot=slot):
+                push(
+                    q_send.at[first + place],
+                    q_recv.at[slot],
+                    q_send_sem,
+                    q_recv_sem.at[step],
+                    device_at(block, place),
+                )
+
+        return carry
+
+    lax.fori_loop(0, early, send_q, 0)
+
     def pack_text(step, carry):
         first = step * span
         normed_keys = normed([text_pad[0, :, tile(first // 2 + at)] for at in pairs], key_gain_both)
@@ -203,50 +248,12 @@
     lax.fori_loop(0, blocks, pack_text, 0)
     text_recv[me] = text_send[me]
 
-    @pl.when(section < sections - 1)
-    def _():
-        pl.semaphore_wait(barrier, seq_count)
-
-    @pl.when(section == sections - 1)
-    def _():
-        pl.semaphore_wait(barrier, seq_count - 1)
-
     def send_text(step, carry):
         target = lax.rem(me + step, seq_count)
         push(text_send.at[target], text_recv.at[me], text_send_sem, text_recv_sem, target)
         return carry
 
     lax.fori_loop(1, seq_count, send_text, 0)
-
-    loads[0].wait()
-
-    def pack_q(step, carry):
-        block = lax.rem(my_block + step * way + blocks, blocks)
-        first = block * span
-        parts = normed([queries[:, tile(tile_index(block, at))].astype(F32) for at in pairs], query_gain_both)
-        for at, data in zip(pairs, parts):
-            data = data.astype(BF16)
-            top, bottom = data[0:half], data[half:]
-            q_send[first + 2 * at] = jnp.where(below_half, top, swap_halves(bottom))
-            q_send[first + 2 * at + 1] = jnp.where(below_half, swap_halves(top), bottom)
-        for turn in turns:
-            place = lax.rem(my_place + turn * way + span, span)
-            slot = step * span + turn
-
-            @pl.when(slot > 0)
-            def _(place=place, slot=slot):
-                push(
-                    q_send.at[first + place],
-                    q_recv.at[slot],
-                    q_send_sem,
-                    q_recv_sem.at[step],
-                    device_at(block, place),
-                )
-
-        return carry
-
-    lax.fori_loop(0, early, pack_q, 0)
-    q_recv[0] = q_send[my_label]
 
     loads[1].wait()
     loads[2].wait()
@@ -279,7 +286,7 @@
     lax.fori_loop(0, blocks, pack_kv, 0)
     kv_recv[0] = kv_send[my_label]
 
-    lax.fori_loop(early, blocks, pack_q, 0)
+    lax.fori_loop(early, blocks, send_q, 0)
 
     @pl.when(section == 0)
     def _():
@@ -484,7 +491,7 @@
 def solution(mesh):
     seq_count = mesh.shape["seq"]
     span = 8
-    early = 6
+    early = 7
 
     def step(
         stale,

time: 73.3 us -> 73.5 us (level); the launches traced: 72 us -> 73.4 us
  Pallas kernels: 71.2 us -> 72.6 us
    pallas_call x1, Pallas kernels: 71.2 us -> 72.6 us  [step(): pl.pallas_call(functools.partial(kernel, seq_count, span, early), out_sha...]
where the time goes in v5:
time: 73.5 us; the launch traced here: 73.4 us
  Pallas kernels  72.6 us (99%)
  local copies, waits for them, and re-layouts  0.83 us (1%)
    pallas_call x1, Pallas kernels, step(): pl.pallas_call(functools.partial(kernel, seq_count, span, early), out_sha...  72.6 us

profile of v5, /device:TPU:1, one launch (start us, length us, event | category | flops | bytes accessed | tf_op | source)
XLA Modules:
  0.0 73.4 jit_solution(4363902763037106492)
XLA Ops:
  0.0 72.6 %joint_attention.1 = bf16[2,64,2432]{2,1,0:T(8,128)(2,1)S(1)} custom-call(s32[2]{0:T(128)} %counts.1, s32[2]{0:T(128)} %bitcast.21, bf16[6,4096]{1,0:T(8,128)(2,1)} %bitcast.18, bf16[6,4096]{1,0:T(8,128)(2,1)} %bitcast.19, f32[1,64]{1,0:T(1,128)} %query_gain_hbm.1, f32[1,64]{1,0:T(1,128)} %key_gain_hbm.1, bf16[38,256]{1,0:T(8,128)(2,1)} %bitcast.20, ...), custom_call_target="tpu_custom_call" | custom-call | tf_op jit(solution)/shard_map/joint_attention/pallas_call | solution.py:520
  72.6 0.8 %copy.15 = bf16[1,2,64,2432]{3,2,1,0:T(8,128)(2,1)} copy(bf16[1,2,64,2432]{3,2,1,0:T(8,128)(2,1)S(1)} %bitcast.12) | data formatting | bytes 1245184
